TPU v7x, 32 devices: a whole 2x2x4 slice. The times are simulated.
32 devices in a mesh: wide: 8 (over z, x), seq: 4 (over y, core).
Axes of the slice: x: 2, y: 2, z: 4, core: 2. Of those that a mesh axis runs over, the one named last changes fastest.
Arguments:
- tokens: bfloat16 [16, 1024, 768], P('wide', 'seq'), may hold values from -6 to 6
- condition: float32 [16, 128], P('wide'), may hold values from -6 to 6
- cotangent: bfloat16 [16, 1024, 768], P('wide', 'seq'), may hold values from -6 to 6
- adaptive: bfloat16 [128, 4608], replicated, may hold values from -0.5 to 0.5
- shifts: float32 [4608], replicated, may hold values from -3 to 3
- prenorm: float32 [768], replicated, may hold values from 0.5 to 1.5
- mixer: bfloat16 [768, 2304], replicated, may hold values from -0.21875 to 0.21875
- projection: bfloat16 [768, 768], replicated, may hold values from -1.25 to 1.25
- postnorm: float32 [768], replicated, may hold values from 0.5 to 1.5
- expand: bfloat16 [768, 3072], replicated, may hold values from -0.21875 to 0.21875
- offsets: float32 [3072], replicated, may hold values from -3 to 3
- contract: bfloat16 [3072, 768], replicated, may hold values from -0.109375 to 0.109375
- baseline: float32 [768], replicated, may hold values from -3 to 3
Outputs:
- layer_output: bfloat16 [16, 1024, 768], P('wide', 'seq')
- grad_tokens: bfloat16 [16, 1024, 768], P('wide', 'seq')
- grad_time: float32 [16, 128], P('wide')
- grad_adaptive: float32 [128, 4608], P('wide')
- grad_shifts: float32 [4608], P('wide')
- grad_prenorm: float32 [768], P('wide')
- grad_mixer: float32 [768, 2304], P('wide')
- grad_projection: float32 [768, 768], P('wide')
- grad_postnorm: float32 [768], P('wide')
- grad_expand: float32 [768, 3072], P('wide')
- grad_offsets: float32 [3072], P('wide')
- grad_contract: float32 [3072, 768], P('wide')
- grad_baseline: float32 [768], P('wide')
All inputs are finite; a program needn't handle non-finite values.
Results may differ from a plain program's by a relative error of at most 0.014.
The roundings to bfloat16 on the way count: a program that leaves them out, or rounds other values in their place, can miss the bound.
Values may be sent and summed in bfloat16 or wider, within the bound.
A program may use at most 192 MiB of HBM per device.

v0:
```python
import math

import jax
import jax.numpy as jnp
from jax import lax
from jax.sharding import PartitionSpec as P

HDIM = 64


epsilon = 1e-06


def layer_norm(values):
    center = values - jnp.mean(values, axis=-1, keepdims=True)
    return center * lax.rsqrt(jnp.mean(center * center, axis=-1, keepdims=True) + epsilon)


def rotary_tables(positions):
    half_dim = HDIM // 2
    frequency = jnp.exp(jnp.arange(half_dim, dtype=jnp.float32) * (-2.0 * math.log(10000.0) / HDIM))
    angles = positions.astype(jnp.float32)[:, None] * frequency[None, :]
    cosines = jnp.concatenate([jnp.cos(angles), jnp.cos(angles)], axis=-1)
    sines = jnp.concatenate([jnp.sin(angles), jnp.sin(angles)], axis=-1)
    return (cosines, sines)


def rotate(values, cosines, sines):
    shaped = values.reshape(values.shape[:-1] + (values.shape[-1] // HDIM, HDIM))
    half_dim = HDIM // 2
    turned = jnp.concatenate([-shaped[..., half_dim:], shaped[..., :half_dim]], axis=-1)
    result = shaped * cosines[..., None, :] + turned * sines[..., None, :]
    return result.reshape(values.shape)


def modulate(inputs, gain, shift, scale):
    return layer_norm(inputs) * gain * (1.0 + scale) + shift


def modulation_of(cond, adaptive_full, shifts):
    return jnp.dot(jax.nn.silu(cond), adaptive_full, precision=lax.Precision.HIGHEST) + shifts


def gelu_tanh(values):
    return jax.nn.gelu(values, approximate=True)


def attend_forward(operands):
    query_row, key_row, value_row = operands
    span = query_row.shape[0]
    length = key_row.shape[0]
    heads_here = query_row.shape[1] // HDIM
    query_heads = query_row.reshape(span, heads_here, HDIM)
    key_heads = key_row.reshape(length, heads_here, HDIM)
    value_heads = value_row.reshape(length, heads_here, HDIM)
    scores = jnp.einsum(
        "qhd,khd->hqk", query_heads, key_heads, preferred_element_type=jnp.float32
    ) * HDIM ** (-0.5)
    maximum = jnp.max(scores, axis=-1, keepdims=True)
    exponent = jnp.exp(scores - maximum)
    totals = jnp.sum(exponent, axis=-1, keepdims=True)
    probability = (exponent / totals).astype(jnp.bfloat16)
    attended = jnp.einsum(
        "hqk,khd->qhd", probability, value_heads, preferred_element_type=jnp.float32
    )
    return (attended.reshape(span, heads_here * HDIM), (maximum + jnp.log(totals))[..., 0])


def attend_backward(operands):
    query_row, key_row, value_row, log_total, grad_row = operands
    span = query_row.shape[0]
    length = key_row.shape[0]
    heads_here = query_row.shape[1] // HDIM
    query_heads = query_row.reshape(span, heads_here, HDIM)
    key_heads = key_row.reshape(length, heads_here, HDIM)
    value_heads = value_row.reshape(length, heads_here, HDIM)
    grad_heads = grad_row.reshape(span, heads_here, HDIM)
    scores = jnp.einsum(
        "qhd,khd->hqk", query_heads, key_heads, preferred_element_type=jnp.float32
    ) * HDIM ** (-0.5)
    probability = jnp.exp(scores - log_total[..., None])
    rounded = probability.astype(jnp.bfloat16)
    grad_values = jnp.einsum(
        "hqk,qhd->khd", rounded, grad_heads, preferred_element_type=jnp.float32
    )
    grad_weights = jnp.einsum(
        "qhd,khd->hqk", grad_heads, value_heads, preferred_element_type=jnp.float32
    )
    inner = jnp.sum(probability * grad_weights, axis=-1, keepdims=True)
    grad_scores = (probability * (grad_weights - inner)).astype(jnp.bfloat16) * jnp.asarray(
        HDIM ** (-0.5), jnp.bfloat16
    )
    grad_queries = jnp.einsum(
        "hqk,khd->qhd", grad_scores, key_heads, preferred_element_type=jnp.float32
    )
    grad_keys = jnp.einsum(
        "hqk,qhd->khd", grad_scores, query_heads, preferred_element_type=jnp.float32
    )
    return (
        grad_queries.reshape(span, heads_here * HDIM),
        grad_keys.reshape(length, heads_here * HDIM),
        grad_values.reshape(length, heads_here * HDIM),
    )


def local(
    tokens,
    condition,
    cotangent,
    adaptive,
    shifts,
    prenorm,
    mixer,
    projection,
    postnorm,
    expand,
    offsets,
    contract,
    baseline,
):
    rows, span, width = tokens.shape
    seq_index = lax.axis_index("seq")
    positions = seq_index * span + jnp.arange(span, dtype=jnp.int32)
    cosines, sines = rotary_tables(positions)
    inputs = tokens.astype(jnp.float32)
    adaptive_full = adaptive.astype(jnp.float32)
    modulation, modulation_back = jax.vjp(modulation_of, condition, adaptive_full, shifts)
    sections = [modulation[:, None, number * width : (number + 1) * width] for number in range(6)]
    shift_attend, scale_attend, gate_attend, shift_feed, scale_feed, gate_feed = sections
    hidden_first, first_back = jax.vjp(modulate, inputs, prenorm, shift_attend, scale_attend)
    hidden_attend = hidden_first.astype(jnp.bfloat16)
    mixed = jnp.dot(
        hidden_attend.reshape(rows * span, width), mixer, preferred_element_type=jnp.float32
    ).reshape(rows, span, 3 * width)
    queries = rotate(mixed[..., :width], cosines, sines).astype(jnp.bfloat16)
    key_rows = rotate(mixed[..., width : 2 * width], cosines, sines).astype(jnp.bfloat16)
    value_rows = mixed[..., 2 * width :].astype(jnp.bfloat16)
    key_whole, value_whole = (
        lax.all_gather(key_rows, "seq", axis=1, tiled=True),
        lax.all_gather(value_rows, "seq", axis=1, tiled=True),
    )
    attended, log_total = lax.map(attend_forward, (queries, key_whole, value_whole))
    attended_low = attended.astype(jnp.bfloat16)
    branch = jnp.dot(
        attended_low.reshape(rows * span, width), projection, preferred_element_type=jnp.float32
    ).reshape(rows, span, width)
    middle = inputs + gate_attend * branch
    hidden_second, second_back = jax.vjp(modulate, middle, postnorm, shift_feed, scale_feed)
    hidden_feed = hidden_second.astype(jnp.bfloat16).reshape(rows * span, width)
    widened = jnp.dot(hidden_feed, expand, preferred_element_type=jnp.float32) + offsets
    activated_full, gelu_back = jax.vjp(gelu_tanh, widened)
    activated = activated_full.astype(jnp.bfloat16)
    narrowed = (
        jnp.dot(activated, contract, preferred_element_type=jnp.float32) + baseline
    ).reshape(rows, span, width)
    layer_output = (middle + gate_feed * narrowed).astype(jnp.bfloat16)
    grad_out = cotangent.astype(jnp.float32)
    grad_gate_feed = jnp.sum(grad_out * narrowed, axis=1, keepdims=True)
    grad_narrowed = (gate_feed * grad_out).astype(jnp.bfloat16).reshape(rows * span, width)
    grad_contract = jnp.dot(activated.T, grad_narrowed, preferred_element_type=jnp.float32)
    grad_baseline = jnp.sum(grad_narrowed, axis=0, dtype=jnp.float32)
    grad_activated = jnp.dot(grad_narrowed, contract.T, preferred_element_type=jnp.float32)
    grad_widened = gelu_back(grad_activated)[0].astype(jnp.bfloat16)
    grad_expand = jnp.dot(hidden_feed.T, grad_widened, preferred_element_type=jnp.float32)
    grad_offsets = jnp.sum(grad_widened, axis=0, dtype=jnp.float32)
    grad_hidden_feed = jnp.dot(grad_widened, expand.T, preferred_element_type=jnp.float32).reshape(
        rows, span, width
    )
    grad_from_second, grad_postnorm, grad_shift_feed, grad_scale_feed = second_back(
        grad_hidden_feed
    )
    grad_middle = grad_out + grad_from_second
    grad_gate_attend = jnp.sum(grad_middle * branch, axis=1, keepdims=True)
    grad_branch = (gate_attend * grad_middle).astype(jnp.bfloat16).reshape(rows * span, width)
    grad_projection = jnp.dot(
        attended_low.reshape(rows * span, width).T, grad_branch, preferred_element_type=jnp.float32
    )
    grad_attended = (
        jnp.dot(grad_branch, projection.T, preferred_element_type=jnp.float32)
        .astype(jnp.bfloat16)
        .reshape(rows, span, width)
    )
    key_again, value_again = (
        lax.all_gather(key_rows, "seq", axis=1, tiled=True),
        lax.all_gather(value_rows, "seq", axis=1, tiled=True),
    )
    grad_queries, grad_keys_whole, grad_values_whole = lax.map(
        attend_backward, (queries, key_again, value_again, log_total, grad_attended)
    )
    grad_keys, grad_values = (
        lax.psum_scatter(grad_keys_whole, "seq", scatter_dimension=1, tiled=True),
        lax.psum_scatter(grad_values_whole, "seq", scatter_dimension=1, tiled=True),
    )
    grad_mixed = (
        jnp.concatenate(
            [
                rotate(grad_queries, cosines, -sines),
                rotate(grad_keys, cosines, -sines),
                grad_values,
            ],
            axis=-1,
        )
        .astype(jnp.bfloat16)
        .reshape(rows * span, 3 * width)
    )
    grad_mixer = jnp.dot(
        hidden_attend.reshape(rows * span, width).T, grad_mixed, preferred_element_type=jnp.float32
    )
    grad_hidden_attend = jnp.dot(grad_mixed, mixer.T, preferred_element_type=jnp.float32).reshape(
        rows, span, width
    )
    grad_from_first, grad_prenorm, grad_shift_attend, grad_scale_attend = first_back(
        grad_hidden_attend
    )
    grad_tokens = (grad_middle + grad_from_first).astype(jnp.bfloat16)
    grad_modulation = jnp.concatenate(
        [
            grad_shift_attend,
            grad_scale_attend,
            grad_gate_attend,
            grad_shift_feed,
            grad_scale_feed,
            grad_gate_feed,
        ],
        axis=-1,
    )[:, 0, :]
    grad_time_local, grad_adaptive, grad_shifts = modulation_back(grad_modulation)
    wide_sums = (
        lax.psum_scatter(grad_adaptive, "wide", scatter_dimension=0, tiled=True),
        lax.psum_scatter(grad_shifts, "wide", scatter_dimension=0, tiled=True),
        lax.psum_scatter(grad_prenorm, "wide", scatter_dimension=0, tiled=True),
        lax.psum_scatter(grad_mixer, "wide", scatter_dimension=0, tiled=True),
        lax.psum_scatter(grad_projection, "wide", scatter_dimension=0, tiled=True),
        lax.psum_scatter(grad_expand, "wide", scatter_dimension=0, tiled=True),
        lax.psum_scatter(grad_offsets, "wide", scatter_dimension=0, tiled=True),
        lax.psum_scatter(grad_contract, "wide", scatter_dimension=0, tiled=True),
        lax.psum_scatter(grad_baseline, "wide", scatter_dimension=0, tiled=True),
        lax.psum_scatter(grad_postnorm, "wide", scatter_dimension=0, tiled=True),
    )
    summed = lax.psum(
        (
            wide_sums[0],
            wide_sums[1],
            wide_sums[2],
            wide_sums[3],
            wide_sums[4],
            wide_sums[5],
            wide_sums[6],
            wide_sums[7],
            wide_sums[8],
            wide_sums[9],
            grad_time_local,
        ),
        "seq",
    )
    return (
        layer_output,
        grad_tokens,
        summed[10],
        summed[0],
        summed[1],
        summed[2],
        summed[3],
        summed[4],
        summed[9],
        summed[5],
        summed[6],
        summed[7],
        summed[8],
    )


def solution(mesh):
    in_specs = (
        P("wide", "seq", None),
        P("wide", None),
        P("wide", "seq", None),
        P(),
        P(),
        P(),
        P(),
        P(),
        P(),
        P(),
        P(),
        P(),
        P(),
    )
    out_specs = (
        P("wide", "seq", None),
        P("wide", "seq", None),
        P("wide", None),
        P("wide", None),
        P("wide"),
        P("wide"),
        P("wide", None),
        P("wide", None),
        P("wide"),
        P("wide", None),
        P("wide"),
        P("wide", None),
        P("wide"),
    )
    return jax.shard_map(local, mesh=mesh, in_specs=in_specs, out_specs=out_specs, check_vma=False)
```

profile of v0, /device:TPU:1, one launch (start us, length us, event | category | flops | bytes accessed | tf_op | source)
XLA Modules:
  0.0 1206.8 jit_solution(5846925060058376679)
XLA Ops:
  65.0 20.0 %all-gather.5.cloned.1.call-done = bf16[2,1024,768]{2,1,0:T(8,128)(2,1)} async-done(((bf16[2,256,768]{2,1,0:T(8,128)(2,1)}), bf16[2,1024,768]{2,1,0:T(8,128)(2,1)}) %all-gather.5.cloned.1.call-update) | async-done | bytes 3145744 | tf_op jit(solution)/shard_map/all_gather | solution.py:139
  89.6 26.1 %while.28 = (s32[]{:T(128)}, bf16[2,256,768]{1,2,0:T(8,128)(2,1)}, f32[2,12,256]{2,1,0:T(8,128)}, bf16[2,1024,768]{1,2,0:T(8,128)(2,1)}, bf16[2,256,768]{1,2,0:T(8,128)(2,1)}, /*index=5*/bf16[2,1024,768]{1,2,0:T(8,128)(2,1)}) while((s32[]{:T(128)}, bf16[2,256,768]{1,2,0:T(8,128)(2,1)}, f32[2,12,256]{2,1,0:T(8,128)}, ...), condition=%wide.region_5.6_spmd.clone, body=%wide.region_2.5_spmd.sunk.clone | while | flops 833614848 | bytes 56144076 | solution.py:142
  126.2 8.6 convolution_add_fusion.1
  134.9 22.3 %convert_reduce_fusion = (f32[3072]{0:T(1024)}, bf16[512,3072]{1,0:T(8,128)(2,1)S(1)}) fusion(f32[512,3072]{1,0:T(8,128)S(1)} %fusion.96, f32[3072]{0:T(1024)S(1)} %copy-done.57, bf16[512,768]{1,0:T(8,128)(2,1)S(1)} %bitcast.213, bf16[3072,768]{1,0:T(8,128)(2,1)S(1)} %bitcast.215), kind=kOutput, calls=%fused_computation.52 | convolution fusion | flops 2452091904 | bytes 14966784 | tf_op jit(solution)/shard_map/dot_general | solution.py:162
  168.7 214.8 %while.29 = (s32[]{:T(128)}, f32[2,256,768]{1,2,0:T(8,128)}, f32[2,1024,768]{2,1,0:T(8,128)}, f32[2,1024,768]{2,1,0:T(8,128)}, bf16[2,1024,768]{1,2,0:T(8,128)(2...) while((s32[]{:T(128)}, f32[2,256,768]{1,2,0:T(8,128)}, ...), condition=%wide.region_12.13_spmd.clone, body=%wide.region_10.12_spmd.sunk.clone | while | flops 2098208768 | bytes 158920944 | solution.py:187
  190.4 27.2 %fusion.189 = f32[12,64,256]{2,1,0:T(8,128)} fusion(bf16[1024,12,64]{0,2,1:T(8,128)(2,1)} %bitcast.181, f32[12,256,1024]{2,1,0:T(8,128)} %fusion.187, f32[12,256,1024]{2,1,0:T(8,128)} %fusion.188, f32[12,256]{1,0:T(8,128)S(1)} %dynamic-slice_bitcast_fusion.3), kind=kOutput, calls=%fused_computation.24.clone.1.clone | convolution fusion | flops 440406016 | bytes 27537408 | tf_op jit(solution)/shard_map/while/body/eval_jaxpr/hqk,khd->qhd/dot_general | solution.py:93
  217.6 34.6 %fusion.191 = f32[12,64,1024]{2,1,0:T(8,128)} fusion(bf16[256,12,64]{0,2,1:T(8,128)(2,1)} %bitcast.189, f32[12,256,1024]{2,1,0:T(8,128)} %fusion.187, f32[12,256,1024]{2,1,0:T(8,128)} %fusion.188, f32[12,256]{1,0:T(8,128)S(1)} %dynamic-slice_bitcast_fusion.3), kind=kOutput, calls=%fused_computation.22.clone.1.clone | convolution fusion | flops 440406016 | bytes 28717056 | tf_op jit(solution)/shard_map/while/body/eval_jaxpr/hqk,qhd->khd/dot_general | solution.py:96
  252.2 8.7 fusion.190
  297.6 27.2 %fusion.189 = f32[12,64,256]{2,1,0:T(8,128)} fusion(bf16[1024,12,64]{0,2,1:T(8,128)(2,1)} %bitcast.181, f32[12,256,1024]{2,1,0:T(8,128)} %fusion.187, f32[12,256,1024]{2,1,0:T(8,128)} %fusion.188, f32[12,256]{1,0:T(8,128)S(1)} %dynamic-slice_bitcast_fusion.3), kind=kOutput, calls=%fused_computation.24.clone.1.clone | convolution fusion | flops 440406016 | bytes 27537408 | tf_op jit(solution)/shard_map/while/body/eval_jaxpr/hqk,khd->qhd/dot_general | solution.py:93
  324.8 34.6 %fusion.191 = f32[12,64,1024]{2,1,0:T(8,128)} fusion(bf16[256,12,64]{0,2,1:T(8,128)(2,1)} %bitcast.189, f32[12,256,1024]{2,1,0:T(8,128)} %fusion.187, f32[12,256,1024]{2,1,0:T(8,128)} %fusion.188, f32[12,256]{1,0:T(8,128)S(1)} %dynamic-slice_bitcast_fusion.3), kind=kOutput, calls=%fused_computation.22.clone.1.clone | convolution fusion | flops 440406016 | bytes 28717056 | tf_op jit(solution)/shard_map/while/body/eval_jaxpr/hqk,qhd->khd/dot_general | solution.py:96
  359.4 8.7 fusion.190
  401.7 40.0 %reduce-scatter.8.cloned.1.call-done = f32[2,256,768]{2,1,0:T(8,128)} async-done(((f32[2,1024,768]{2,1,0:T(8,128)}), f32[2,256,768]{2,1,0:T(8,128)}) %reduce-scatter.8.cloned.1.call-update) | async-done | bytes 1572880 | tf_op jit(solution)/shard_map/reduce_scatter | solution.py:191
  450.5 52.1 %reduce-scatter.10.cloned.1.call-done = f32[2,256,768]{2,1,0:T(8,128)} async-done(((f32[2,1024,768]{2,1,0:T(8,128)}), f32[2,256,768]{2,1,0:T(8,128)}) %reduce-scatter.10.cloned.1.call-update) | async-done | bytes 1572880 | tf_op jit(solution)/shard_map/reduce_scatter | solution.py:192
  518.7 10.4 fusion.88
  529.1 8.4 fusion.98
  537.7 7.0 convolution_bitcast_fusion
  544.7 29.2 %reduce-scatter.16.cloned.1.call-done = f32[96,768]{1,0:T(8,128)} async-done(((f32[768,768]{1,0:T(8,128)}), f32[96,768]{1,0:T(8,128)}) %reduce-scatter.16.cloned.1.call-update) | async-done | bytes 294928 | tf_op jit(solution)/shard_map/reduce_scatter | solution.py:233
  573.9 71.4 %reduce-scatter.12.cloned.1.call-done = f32[16,4608]{1,0:T(8,128)} async-done(((f32[128,4608]{1,0:T(8,128)}), f32[16,4608]{1,0:T(8,128)}) %reduce-scatter.12.cloned.1.call-update) | async-done | bytes 294928 | tf_op jit(solution)/shard_map/reduce_scatter | solution.py:229
  645.4 167.2 %reduce-scatter.20.cloned.1.call-done = f32[384,768]{1,0:T(8,128)} async-done(((f32[3072,768]{1,0:T(8,128)}), f32[384,768]{1,0:T(8,128)}) %reduce-scatter.20.cloned.1.call-update) | async-done | bytes 1179664 | tf_op jit(solution)/shard_map/reduce_scatter | solution.py:236
  812.6 166.2 %reduce-scatter.18.cloned.1.call-done = f32[96,3072]{1,0:T(8,128)} async-done(((f32[768,3072]{1,0:T(8,128)}), f32[96,3072]{1,0:T(8,128)}) %reduce-scatter.18.cloned.1.call-update) | async-done | bytes 1179664 | tf_op jit(solution)/shard_map/reduce_scatter | solution.py:234
  978.8 130.9 %reduce-scatter.14.cloned.1.call-done = f32[96,2304]{1,0:T(8,128)} async-done(((f32[768,2304]{1,0:T(8,128)}), f32[96,2304]{1,0:T(8,128)}) %reduce-scatter.14.cloned.1.call-update) | async-done | bytes 884752 | tf_op jit(solution)/shard_map/reduce_scatter | solution.py:232
  1114.3 30.0 %all-reduce.5 = (f32[4608]{0:T(1024)}, f32[768]{0:T(1024)}, f32[768]{0:T(1024)}, f32[3072]{0:T(1024)}, f32[768]{0:T(1024)}) all-reduce(f32[4608]{0:T(1024)} %reduce_sum.231, f32[768]{0:T(1024)S(1)} %copy-done.52, f32[768]{0:T(1024)S(1)} %copy-done.51, ...), channel_id=5, replica_groups=mesh['wide'=8,'seq'=4] {'wide'}, use_global_device_ids=true, to_apply=%region_27.28.clone | all-reduce | flops 9984 | bytes 79872
  1152.0 13.9 %all-reduce.6 = (f32[2,128]{1,0:T(2,128)}, f32[576]{0:T(1024)}, f32[96]{0:T(128)}, f32[96]{0:T(128)}, f32[384]{0:T(512)}, /*index=5*/f32[96]{0:T(128)}) all-reduce(f32[2,128]{1,0:T(2,128)S(1)} %fusion.80, f32[576]{0:T(1024)S(1)} %dynamic-slice.1, f32[96]{0:T(128)} %dynamic-slice.3, ...), channel_id=1, replica_groups=mesh['wide'=8,'seq'=4] {'seq'}, use_global_device_ids=true, to_apply=%region_23.24 | all-reduce | flops 1504 | bytes 12032 | tf_op jit(solution)/shard_map/psum | solution.py:240
  1165.9 27.2 %all-reduce.10.cloned.1.call-done = (f32[16,4608]{1,0:T(8,128)}, f32[96,2304]{1,0:T(8,128)}, f32[96,768]{1,0:T(8,128)}, f32[96,3072]{1,0:T(8,128)}, f32[384,768]{1,0:T(8,128)}) async-done(((f32[16,4608]{1,0:T(8,128)}, f32[96,2304]{1,0:T(8,128)}, f32[96,768]{1,0:T(8,128)}, f32[96,3072]{1,0:T(8,128)}, f32[384,768]{1,0:T(8,128)}), (f32[16,4608]{1,0:T(8,128)}, f32[96,2304]{1,0:T(8,128)}, f32[96,768]{1,0:T(8,128)}, ...) | async-done | bytes 3833872 | tf_op jit(solution)/shard_map/psum | solution.py:240
  (290 shorter events, 243.2 us)
Async XLA Ops:
  7.2 5.6 copy-start
  7.2 53.0 %all-gather.3.cloned.1.call-start = ((), (), s32[]{:S(2)}) async-start(), calls=%async_computation.7 | async-start | bytes 3932160 | tf_op jit(solution)/shard_map/all_gather | solution.py:140
  8.8 6.3 copy-start.36
  18.2 66.8 %all-gather.5.cloned.1.call-start = ((), (), s32[]{:S(2)}) async-start(), calls=%async_computation.8 | async-start | bytes 3932160 | tf_op jit(solution)/shard_map/all_gather | solution.py:139
  53.7 387.9 %reduce-scatter.8.cloned.1.call-start = ((), (), s32[]{:S(2)}) async-start(), calls=%async_computation.9 | async-start | bytes 7864320 | tf_op jit(solution)/shard_map/reduce_scatter | solution.py:191
  121.5 13.3 %slice-start.2 = ((s8[4718592]{0:T(1024)(128)(4,1)}), s8[4194304]{0:T(1024)(128)(4,1)S(1)}, s32[]{:S(2)}) async-start(s8[4718592]{0:T(1024)(128)(4,1)} %bitcast.214), calls=%async_computation.19 | async-start | bytes 8388608
  126.1 8.7 copy-start.14
  126.1 8.7 copy-start.26
  126.1 8.7 slice-start.3
  126.2 30.9 %slice-start = ((s8[4718592]{0:T(1024)(128)(4,1)}), s8[4194304]{0:T(1024)(128)(4,1)S(1)}, s32[]{:S(2)}) async-start(s8[4718592]{0:T(1024)(128)(4,1)} %bitcast.206), calls=%async_computation.17 | async-start | bytes 8388608
  134.8 26.6 %copy-start.16 = (f32[512,768]{1,0:T(8,128)}, f32[512,768]{1,0:T(8,128)S(1)}, u32[]{:S(2)}) copy-start(f32[512,768]{1,0:T(8,128)S(1)} %convolution_add_fusion.1) | copy-start | bytes 4718596
  134.8 22.3 %slice-start.1 = ((s8[4718592]{0:T(1024)(128)(4,1)}), s8[524288]{0:T(1024)(128)(4,1)S(1)}, s32[]{:S(2)}) async-start(s8[4718592]{0:T(1024)(128)(4,1)} %bitcast.206), calls=%async_computation.18 | async-start | bytes 1048576
  174.2 9.9 copy-start.4
  176.8 7.2 copy-start.1
  281.4 9.9 copy-start.4
  284.0 7.2 copy-start.1
  383.6 119.0 %reduce-scatter.10.cloned.1.call-start = ((), (), s32[]{:S(2)}) async-start(), calls=%async_computation.10 | async-start | bytes 7864320 | tf_op jit(solution)/shard_map/reduce_scatter | solution.py:192
  384.2 189.8 %reduce-scatter.16.cloned.1.call-start = ((), (), s32[]{:S(2)}) async-start(), calls=%async_computation.13 | async-start | bytes 2654208 | tf_op jit(solution)/shard_map/reduce_scatter | solution.py:233
  395.8 249.6 %reduce-scatter.12.cloned.1.call-start = ((), (), s32[]{:S(2)}) async-start(), calls=%async_computation.11 | async-start | bytes 2654208 | tf_op jit(solution)/shard_map/reduce_scatter | solution.py:229
  518.4 294.1 %reduce-scatter.20.cloned.1.call-start = ((), (), s32[]{:S(2)}) async-start(), calls=%async_computation.15 | async-start | bytes 10616832 | tf_op jit(solution)/shard_map/reduce_scatter | solution.py:236
  529.1 449.7 %reduce-scatter.18.cloned.1.call-start = ((), (), s32[]{:S(2)}) async-start(), calls=%async_computation.14 | async-start | bytes 10616832 | tf_op jit(solution)/shard_map/reduce_scatter | solution.py:234
  537.6 572.1 %reduce-scatter.14.cloned.1.call-start = ((), (), s32[]{:S(2)}) async-start(), calls=%async_computation.12 | async-start | bytes 7962624 | tf_op jit(solution)/shard_map/reduce_scatter | solution.py:232
  544.7 648.4 %all-reduce.10.cloned.1.call-start = ((), (), s32[]{:S(2)}) async-start(), calls=%async_computation.16 | async-start | bytes 7667712 | tf_op jit(solution)/shard_map/psum | solution.py:240
  1109.7 40.0 %copy-start.55 = (f32[2,128]{1,0:T(2,128)S(1)}, f32[2,128]{1,0:T(2,128)}, u32[]{:S(2)}) copy-start(f32[2,128]{1,0:T(2,128)} %param.18) | copy-start | bytes 3076
  (57 other events, 152.4 us)
Sparse Core Ops, SparseCore 0:
  18.3 31.0 all-gather.2
  53.9 31.0 all-gather.4
  383.7 57.9 reduce-scatter.7
  444.2 58.3 reduce-scatter.9
  505.9 67.9 reduce-scatter.15
  577.3 68.0 reduce-scatter.11
  649.0 163.5 reduce-scatter.19
  816.2 162.5 reduce-scatter.17
  982.5 127.1 reduce-scatter.13
  1112.5 80.5 all-reduce.9
where the time goes:
time: 1220 us; the launch traced here: 1210 us
  waiting for transfers between devices  705 us (58%)
  matrix products  263 us (22%)
  local copies, waits for them, and re-layouts  129 us (11%)
  other arithmetic  47.9 us (4%)
  blocking collectives  43.9 us (4%)
  between operations  17.1 us (1%)
    reduce_scatter x1, waiting for transfers between devices, local(): lax.psum_scatter(grad_contract, 'wide', scatter_dimension=0, tiled=True)  167 us
    reduce_scatter x1, waiting for transfers between devices, local(): lax.psum_scatter(grad_expand, 'wide', scatter_dimension=0, tiled=True)  166 us
    reduce_scatter x1, waiting for transfers between devices, local(): lax.psum_scatter(grad_mixer, 'wide', scatter_dimension=0, tiled=True)  131 us
    reduce_scatter x1, waiting for transfers between devices, local(): lax.psum_scatter(grad_adaptive, 'wide', scatter_dimension=0, tiled=True)  71.4 us
    dot_general x2, matrix products, attend_backward(): jnp.einsum('hqk,qhd->khd', grad_scores, query_heads, preferred_element_ty...  69.2 us
    dot_general x2, matrix products, attend_backward(): jnp.einsum('hqk,khd->qhd', grad_scores, key_heads, preferred_element_type...  54.5 us
    reduce_scatter x1, waiting for transfers between devices, local(): lax.psum_scatter(grad_values_whole, 'seq', scatter_dimension=1, tiled=True)  52.1 us
    reduce_scatter x1, waiting for transfers between devices, local(): lax.psum_scatter(grad_keys_whole, 'seq', scatter_dimension=1, tiled=True)  40 us
  transfers between devices with their start and end apart: 10, of which 9 were waited for; matrix products, arithmetic and copies ran while one was open for 10% of the time, Pallas kernels for 0%

commit v1 on v0

v1 whole, which is shorter than its diff:
```python
import functools
import math

import jax
import jax.numpy as jnp
import numpy as np
from jax import lax
from jax.experimental import pallas as pl
from jax.experimental.pallas import tpu as pltpu
from jax.sharding import PartitionSpec as P

F32 = jnp.float32
BF16 = jnp.bfloat16
MESH = pl.DeviceIdType.MESH
HDIM = 64
PAIR = 2 * HDIM
EPSILON = 1e-06
GELU_A = 0.7978845608
GELU_B = 0.044715

ROWS_BY_ROWS = (((1,), (1,)), ((), ()))
COLS_BY_COLS = (((0,), (0,)), ((), ()))


def dot(a, b, dims=None):
    if dims is None:
        return jnp.dot(a, b, preferred_element_type=F32)
    return lax.dot_general(a, b, dims, preferred_element_type=F32)


def normalize(values):
    center = values - jnp.mean(values, axis=-1, keepdims=True)
    scale = lax.rsqrt(jnp.mean(center * center, axis=-1, keepdims=True) + EPSILON)
    return center * scale, scale


def normalize_back(grad, normal, scale):
    first = jnp.mean(grad, axis=-1, keepdims=True)
    second = jnp.mean(grad * normal, axis=-1, keepdims=True)
    return scale * (grad - first - normal * second)


def turn(values):
    lane = lax.broadcasted_iota(jnp.int32, values.shape, 1)
    first = lax.rem(lane, HDIM) < HDIM // 2
    return jnp.where(
        first, pltpu.roll(values, PAIR - HDIM // 2, 1), pltpu.roll(values, HDIM // 2, 1)
    )


def column_sum(values):
    return jnp.sum(values, axis=0, keepdims=True)


def layer_kernel(
    tok_h, cot_h, adap_h, mix_h, proj_h, exp_h, con_h,
    cond, shifts, prenorm, postnorm, offsets, baseline, cosine, sine,
    out_h, gtok_h, ge_h, gc_h, gp_h, gm_h, vec_h, e_h,
    tok, cot, adap, mix, proj, exp, con, mod, hid_a, qm, kk, vv, v_t, k_t, est, inv_l, att_t, att_s, att,
    branch, middle, hid_f, gnar, gbr, act, gwid, nacc, hacc, nsend, nrecv, hsend, hrecv,
    dom, dsum, dv, dk, dq_t, gmx, ost, ge, gc, gp, gm, vec,
    lsem, esem, ssem, rsem,
):
    span = tok.shape[1]
    width = tok.shape[2]
    total = hid_a.shape[0]
    half = width // 2
    pairs = half // PAIR
    blocks = total // span
    ub = exp.shape[1] // 2
    w = lax.axis_index("wide")
    s = lax.axis_index("seq")
    y = lax.div(s, 2)
    c = lax.rem(s, 2)
    core_dev = (w, y * 2 + 1 - c)
    y_dev = (w, (1 - y) * 2 + c)

    def rows_of(p):
        return pl.ds(pl.multiple_of(p * span, span), span)

    def remote(src, dst, k, dev):
        return pltpu.make_async_remote_copy(
            src_ref=src, dst_ref=dst, send_sem=ssem.at[k], recv_sem=rsem.at[k],
            device_id=dev, device_id_type=MESH,
        )

    def local(src, dst, k):
        return pltpu.make_async_copy(src, dst, lsem.at[k])

    loads = [local(adap_h, adap, 0), local(tok_h.at[y], tok.at[y], 1), local(cot_h.at[y], cot.at[y], 2)]
    mix_loads = []
    for j in range(pairs):
        for b in range(3):
            mix_loads.append(local(
                mix_h.at[:, pl.ds(pl.multiple_of(b * width + c * half + j * PAIR, PAIR), PAIR)],
                mix.at[:, pl.ds((j * 3 + b) * PAIR, PAIR)],
                3 + j * 3 + b,
            ))
    k0 = 3 + 3 * pairs
    proj_load = local(proj_h, proj, k0)
    exp_load = local(exp_h.at[:, pl.ds(pl.multiple_of(c * 2 * ub, PAIR), 2 * ub)], exp, k0 + 1)
    con_load = local(con_h.at[pl.ds(pl.multiple_of(c * 2 * ub, PAIR), 2 * ub), :], con, k0 + 2)
    for item in loads + mix_loads + [proj_load, exp_load, con_load]:
        item.start()

    barrier = pltpu.get_barrier_semaphore()
    for dev in (core_dev, y_dev):
        pl.semaphore_signal(barrier, inc=1, device_id=dev, device_id_type=MESH)
    pl.semaphore_wait(barrier, 2)

    tok_swap = remote(tok_h.at[1 - y], tok.at[y], 0, y_dev)
    cot_swap = remote(cot_h.at[1 - y], cot.at[y], 1, y_dev)
    tok_swap.start()
    cot_swap.start()

    vec[...] = jnp.zeros_like(vec)

    loads[0].wait()
    crow = jnp.where(y == 0, cond[0:1, :], cond[1:2, :])
    crow = crow * (1.0 / (1.0 + jnp.exp(-crow)))
    extent = crow.shape[1]
    eye = lax.broadcasted_iota(jnp.int32, (extent, extent), 0) == lax.broadcasted_iota(
        jnp.int32, (extent, extent), 1
    )
    ccol = jnp.sum(jnp.where(eye, jnp.broadcast_to(crow, (extent, extent)), 0.0), axis=1, keepdims=True)
    for n in range(6):
        part = pl.ds(n * width, width)
        mod[n : n + 1, :] = column_sum(adap[:, part].astype(F32) * ccol) + shifts[:, part]

    def first_norm(j, t):
        normal, _ = normalize(tok[j].astype(F32))
        value = normal * (prenorm[...] * (1.0 + mod[1:2, :])) + mod[0:1, :]
        place = rows_of(2 * j + c)
        hid_a[place, :] = value.astype(BF16)
        push = remote(hid_a.at[place, :], hid_a.at[place, :], 2 + t, core_dev)
        push.start()

    def wait_hid_a(j, t):
        place = rows_of(2 * j + 1 - c)
        remote(hid_a.at[place, :], hid_a.at[place, :], 2 + t, core_dev).wait_recv()

    def project(p):
        place = rows_of(p)
        mixed = dot(hid_a[place, :], mix[...])
        cos_here = cosine[place, :]
        sin_here = sine[place, :]
        lane = lax.broadcasted_iota(jnp.int32, (span, PAIR), 1)
        for j in range(pairs):
            base = j * 3 * PAIR
            query = mixed[:, base : base + PAIR]
            query = (query * cos_here + turn(query) * sin_here).astype(BF16) * jnp.asarray(
                HDIM ** (-0.5), BF16
            )
            zero = jnp.zeros_like(query)
            qm[2 * j, place, :] = jnp.where(lane < HDIM, query, zero)
            qm[2 * j + 1, place, :] = jnp.where(lane < HDIM, zero, query)
            key = mixed[:, base + PAIR : base + 2 * PAIR]
            kk[j, place, :] = (key * cos_here + turn(key) * sin_here).astype(BF16)
            vv[j, place, :] = mixed[:, base + 2 * PAIR : base + 3 * PAIR].astype(BF16)

    loads[1].wait()
    first_norm(y, 0)
    for item in mix_loads:
        item.wait()
    project(2 * y + c)
    tok_swap.wait_recv()
    first_norm(1 - y, 1)
    wait_hid_a(y, 0)
    project(2 * y + 1 - c)
    project(2 * (1 - y) + c)
    wait_hid_a(1 - y, 1)
    project(2 * (1 - y) + 1 - c)
    for j in range(pairs):
        k_t[j * PAIR : (j + 1) * PAIR, :] = kk[j].T
        v_t[j * PAIR : (j + 1) * PAIR, :] = vv[j].T

    loads[2].wait()
    cot_swap.wait_recv()
    for j in range(2):
        place = rows_of(2 * j + c)
        low = (cot[j].astype(F32) * mod[5:6, :]).astype(BF16)
        gnar[place, :] = low
        vec[8:9, :] += column_sum(low.astype(F32))
        remote(gnar.at[place, :], gnar.at[place, :], 4 + j, core_dev).start()

    def e_copy(n, slot):
        return pltpu.make_async_copy(est.at[slot], e_h.at[n], esem.at[slot])

    def attend(j, carry):
        for hh in range(2):
            h = 2 * j + hh
            head = pl.ds(pl.multiple_of(h * HDIM, HDIM), HDIM)
            for qb in range(blocks):
                n = h * blocks + qb
                slot = qb % 2
                part = pl.ds(qb * span, span)
                score = dot(kk[j], qm[h, part, :], ROWS_BY_ROWS)
                top = jnp.max(score, axis=0, keepdims=True)
                value = jnp.exp(score - top)
                inverse = 1.0 / column_sum(value)
                low = value.astype(BF16)
                if hh == 0 and qb < 2:
                    @pl.when(j > 0)
                    def _():
                        e_copy(n, slot).wait()
                else:
                    e_copy(n, slot).wait()
                est[slot] = low
                e_copy(n, slot).start()
                inv_l[pl.ds(h, 1), part] = inverse
                att_t[head, part] = (dot(v_t[head, :], low) * inverse).astype(BF16)
        here = att_t[pl.ds(pl.multiple_of(j * PAIR, PAIR), PAIR), :].T
        att_s[j] = here
        lanes = pl.ds(pl.multiple_of(c * half + j * PAIR, PAIR), PAIR)
        for jj in range(2):
            att[jj, :, lanes] = att_s[j, rows_of(2 * jj + c), :]
            remote(
                att_s.at[j, rows_of(2 * jj + 1 - c), :], att.at[jj, :, lanes], 6 + 2 * j + jj, core_dev
            ).start()
        return carry

    lax.fori_loop(0, pairs, attend, 0)
    for slot in range(2):
        e_copy(0, slot).wait()
    k1 = 6 + 2 * pairs
    for j in range(pairs):
        lanes = pl.ds(pl.multiple_of((1 - c) * half + j * PAIR, PAIR), PAIR)
        for jj in range(2):
            remote(
                att_s.at[j, rows_of(2 * jj + 1 - c), :], att.at[jj, :, lanes], 6 + 2 * j + jj, core_dev
            ).wait_recv()

    proj_load.wait()
    for j in range(2):
        grown = dot(att[j], proj[...])
        branch[j] = grown
        value = tok[j].astype(F32) + mod[2:3, :] * grown
        middle[j] = value
        normal, _ = normalize(value)
        place = rows_of(2 * j + c)
        hid_f[place, :] = (
            normal * (postnorm[...] * (1.0 + mod[4:5, :])) + mod[3:4, :]
        ).astype(BF16)
        remote(hid_f.at[place, :], hid_f.at[place, :], k1 + j, core_dev).start()

    exp_load.wait()
    con_load.wait()
    for i in range(2):
        units = pl.ds(i * ub, ub)
        off_units = pl.ds(pl.multiple_of((2 * c + i) * ub, PAIR), ub)

        def feed(t, carry, i=i, units=units, off_units=off_units):
            late = lax.div(t, 2)
            j = lax.rem(t, 2)
            p = 2 * j + lax.rem(c + late + i, 2)
            place = rows_of(p)
            if i == 0:
                @pl.when(late == 1)
                def _():
                    remote(hid_f.at[place, :], hid_f.at[place, :], k1 + j, core_dev).wait_recv()
                    remote(gnar.at[place, :], gnar.at[place, :], 4 + j, core_dev).wait_recv()
            v = dot(hid_f[place, :], exp[:, units]) + offsets[:, off_units]
            square = v * v
            th = jnp.tanh(v * (GELU_A + (GELU_A * GELU_B) * square))
            up = 0.5 + 0.5 * th
            low = (v * up).astype(BF16)
            act[place, :] = low
            slope = up + (v * (0.5 - 0.5 * th * th)) * (GELU_A + (3.0 * GELU_A * GELU_B) * square)
            grad = (dot(gnar[place, :], con[units, :], ROWS_BY_ROWS) * slope).astype(BF16)
            gwid[place, :] = grad
            r = 9 + 2 * c + i
            vec[pl.ds(r, 1), :] += column_sum(grad.astype(F32))
            n_part = dot(low, con[units, :])
            h_part = dot(grad, exp[:, units], ROWS_BY_ROWS)
            if i == 0:
                nacc[place, :] = n_part
                hacc[place, :] = h_part
            else:
                n_part = nacc[place, :] + n_part
                h_part = hacc[place, :] + h_part
                nacc[place, :] = n_part
                hacc[place, :] = h_part

                @pl.when(late == 0)
                def _():
                    hsend[j] = hacc[place, :].astype(BF16)
                    remote(hsend.at[j], hrecv.at[j], k1 + 2 + j, core_dev).start()
                    nsend[j] = nacc[place, :].astype(BF16)
                    remote(nsend.at[j], nrecv.at[j], k1 + 4 + j, core_dev).start()
            return carry

        lax.fori_loop(0, 4, feed, 0)
        ge[:, units] = dot(hid_f[...], gwid[...], COLS_BY_COLS).astype(BF16)
        gc[units, :] = dot(act[...], gnar[...], COLS_BY_COLS).astype(BF16)

    for j in range(2):
        remote(hsend.at[j], hrecv.at[j], k1 + 2 + j, core_dev).wait_recv()
        place = rows_of(2 * j + c)
        got = hacc[place, :] + hrecv[j].astype(F32)
        normal, scale = normalize(middle[j])
        vec[3:4, :] += column_sum(got)
        both = column_sum(got * normal)
        vec[4:5, :] += both * postnorm[...]
        vec[7:8, :] += both * (1.0 + mod[4:5, :])
        g = cot[j].astype(F32)
        remote(nsend.at[j], nrecv.at[j], k1 + 4 + j, core_dev).wait_recv()
        narrowed = nacc[place, :] + nrecv[j].astype(F32) + baseline[...]
        ost[j] = (middle[j] + mod[5:6, :] * narrowed).astype(BF16)
        vec[5:6, :] += column_sum(g * narrowed)
        value = g + normalize_back(got * (postnorm[...] * (1.0 + mod[4:5, :])), normal, scale)
        middle[j] = value
        vec[2:3, :] += column_sum(value * branch[j])
        gbr[place, :] = (mod[2:3, :] * value).astype(BF16)
        remote(gbr.at[place, :], gbr.at[place, :], k1 + 6 + j, core_dev).start()

    out_local = local(ost.at[y], out_h.at[y], 0)
    out_push = remote(ost.at[1 - y], out_h.at[y], k1 + 8, y_dev)
    out_local.start()
    out_push.start()
    for j in range(2):
        place = rows_of(2 * j + 1 - c)
        remote(gbr.at[place, :], gbr.at[place, :], k1 + 6 + j, core_dev).wait_recv()

    def e_back(n, slot):
        return pltpu.make_async_copy(e_h.at[n], est.at[slot], esem.at[slot])

    e_back(0, 0).start()
    gp[...] = dot(att_t[...], gbr[...]).astype(BF16)

    def attend_back(j, carry):
        pair = pl.ds(pl.multiple_of(j * PAIR, PAIR), PAIR)
        own = proj[pl.ds(pl.multiple_of(c * half + j * PAIR, PAIR), PAIR), :]
        grown = dot(own, gbr[...], ROWS_BY_ROWS).astype(BF16).astype(F32)
        here = att_t[pair, :].astype(F32)
        scaled = []
        for hh in range(2):
            inverse = inv_l[pl.ds(2 * j + hh, 1), :]
            rows = slice(hh * HDIM, (hh + 1) * HDIM)
            dsum[hh : hh + 1, :] = column_sum(grown[rows] * here[rows]) * inverse
            scaled.append(grown[rows] * inverse)
        turned = jnp.concatenate(scaled, axis=0).astype(BF16).T
        lane = lax.broadcasted_iota(jnp.int32, turned.shape, 1)
        zero = jnp.zeros_like(turned)
        dom[0] = jnp.where(lane < HDIM, turned, zero)
        dom[1] = jnp.where(lane < HDIM, zero, turned)
        for hh in range(2):
            h = 2 * j + hh
            head = pl.ds(pl.multiple_of(h * HDIM, HDIM), HDIM)
            for qb in range(blocks):
                n = h * blocks + qb
                slot = qb % 2
                e_back(n, slot).wait()
                if hh == 1 and qb == blocks - 1:
                    @pl.when(j < pairs - 1)
                    def _():
                        e_back(n + 1, 1 - slot).start()
                else:
                    e_back(n + 1, 1 - slot).start()
                part = pl.ds(qb * span, span)
                low = est[slot]
                there = dom[hh, part, :]
                grad = dot(vv[j], there, ROWS_BY_ROWS)
                grad = (low.astype(F32) * (grad - dsum[hh : hh + 1, part])).astype(BF16)
                v_part = dot(low, there)
                k_part = dot(grad, qm[h, part, :])
                if hh == 0 and qb == 0:
                    dv[...] = v_part
                    dk[...] = k_part
                else:
                    dv[...] += v_part
                    dk[...] += k_part
                dq_t[hh * HDIM : (hh + 1) * HDIM, part] = dot(k_t[head, :], grad)
        gq = dq_t[...].T * HDIM ** (-0.5)
        gk = dk[...]
        gmx[:, :PAIR] = (gq * cosine[...] - turn(gq) * sine[...]).astype(BF16)
        gmx[:, PAIR : 2 * PAIR] = (gk * cosine[...] - turn(gk) * sine[...]).astype(BF16)
        gmx[:, 2 * PAIR :] = dv[...].astype(BF16)
        gm[j] = dot(hid_a[...], gmx[...], COLS_BY_COLS).astype(BF16)
        lanes = pl.ds(pl.multiple_of(j * 3 * PAIR, PAIR), 3 * PAIR)

        def back(p, inner):
            place = rows_of(p)
            part = dot(gmx[place, :], mix[:, lanes], ROWS_BY_ROWS)

            @pl.when(j == 0)
            def _():
                hacc[place, :] = part

            @pl.when(j > 0)
            def _():
                hacc[place, :] += part

            return inner

        lax.fori_loop(0, blocks, back, 0)
        return carry

    lax.fori_loop(0, pairs, attend_back, 0)
    for j in range(2):
        remote(hsend.at[j], hrecv.at[j], k1 + 2 + j, core_dev).wait_send()
        hsend[j] = hacc[rows_of(2 * j + 1 - c), :].astype(BF16)
        remote(hsend.at[j], hrecv.at[j], k1 + 9 + j, core_dev).start()

    out_local.wait()
    out_push.wait()
    for j in range(2):
        remote(hsend.at[j], hrecv.at[j], k1 + 9 + j, core_dev).wait_recv()
        got = hacc[rows_of(2 * j + c), :] + hrecv[j].astype(F32)
        normal, scale = normalize(tok[j].astype(F32))
        vec[0:1, :] += column_sum(got)
        both = column_sum(got * normal)
        vec[1:2, :] += both * prenorm[...]
        vec[6:7, :] += both * (1.0 + mod[1:2, :])
        ost[j] = (
            middle[j] + normalize_back(got * (prenorm[...] * (1.0 + mod[1:2, :])), normal, scale)
        ).astype(BF16)
    gtok_local = local(ost.at[y], gtok_h.at[y], 0)
    gtok_push = remote(ost.at[1 - y], gtok_h.at[y], k1 + 11, y_dev)
    gtok_local.start()
    gtok_push.start()
    stores = [local(ge, ge_h, 1), local(gc, gc_h, 2), local(gp, gp_h, 3), local(gm, gm_h, 4), local(vec, vec_h, 5)]
    for item in stores:
        item.start()
    for item in stores:
        item.wait()
    gtok_local.wait()
    gtok_push.wait()

    tok_swap.wait_send()
    cot_swap.wait_send()
    for j in range(2):
        place = rows_of(2 * j + c)
        for k in (2 + j, 4 + j, k1 + j, k1 + 6 + j):
            remote(hid_a.at[place, :], hid_a.at[place, :], k, core_dev).wait_send()
        for k in (k1 + 4 + j, k1 + 9 + j):
            remote(hsend.at[j], hrecv.at[j], k, core_dev).wait_send()
    for j in range(pairs):
        for jj in range(2):
            remote(
                att_s.at[j, rows_of(2 * jj), :], att.at[jj, :, pl.ds(0, PAIR)], 6 + 2 * j + jj, core_dev
            ).wait_send()


def rotary_constants(length):
    half_dim = HDIM // 2
    frequency = np.exp(np.arange(half_dim, dtype=np.float32) * np.float32(-2.0 * math.log(10000.0) / HDIM))
    angles = np.arange(length, dtype=np.float32)[:, None] * frequency[None, :].astype(np.float32)
    angles = angles.astype(np.float64)
    cosine = np.cos(angles).astype(np.float32)
    sine = np.sin(angles).astype(np.float32)
    cosine = np.concatenate([cosine] * 4, axis=-1)
    sine = np.concatenate([-sine, sine, -sine, sine], axis=-1)
    return cosine, sine


def local_part(wide_count, tokens, condition, cotangent, adaptive, shifts, prenorm, mixer, projection, postnorm,
               expand, offsets, contract, baseline):
    rows, span, width = tokens.shape
    total = 4 * span
    half = width // 2
    pairs = half // PAIR
    ff = expand.shape[1]
    uf = ff // 2
    ub = uf // 2
    cosine, sine = rotary_constants(total)
    hbm = pl.BlockSpec(memory_space=pl.ANY)
    vmem = pl.BlockSpec(memory_space=pltpu.VMEM)
    row_of = lambda v: v.reshape(1, -1)
    out_shape = (
        jax.ShapeDtypeStruct(tokens.shape, BF16),
        jax.ShapeDtypeStruct(tokens.shape, BF16),
        jax.ShapeDtypeStruct((width, uf), BF16),
        jax.ShapeDtypeStruct((uf, width), BF16),
        jax.ShapeDtypeStruct((half, width), BF16),
        jax.ShapeDtypeStruct((pairs, width, 3 * PAIR), BF16),
        jax.ShapeDtypeStruct((16, width), F32),
        jax.ShapeDtypeStruct((2 * pairs * 4, total, span), BF16),
    )
    V = pltpu.VMEM
    piece = (2, span, width)
    whole = (total, width)
    scratch = [
        V(piece, BF16), V(piece, BF16), V(adaptive.shape, BF16), V((width, 3 * half), BF16),
        V(projection.shape, BF16), V((width, uf), BF16), V((uf, width), BF16), V((8, width), F32),
        V(whole, BF16), V((2 * pairs, total, PAIR), BF16), V((pairs, total, PAIR), BF16),
        V((pairs, total, PAIR), BF16), V((half, total), BF16), V((half, total), BF16),
        V((2, total, span), BF16), V((8, total), F32), V((half, total), BF16), V((pairs, total, PAIR), BF16),
        V(piece, BF16),
        V(piece, F32), V(piece, F32), V(whole, BF16), V(whole, BF16), V(whole, BF16), V((total, ub), BF16),
        V((total, ub), BF16), V(whole, F32), V(whole, F32), V(piece, BF16), V(piece, BF16), V(piece, BF16),
        V(piece, BF16),
        V((2, total, PAIR), BF16), V((8, total), F32), V((total, PAIR), F32), V((total, PAIR), F32),
        V((PAIR, total), F32), V((total, 3 * PAIR), BF16), V(piece, BF16),
        V((width, uf), BF16), V((uf, width), BF16), V((half, width), BF16), V((pairs, width, 3 * PAIR), BF16),
        V((16, width), F32),
        pltpu.SemaphoreType.DMA((16,)), pltpu.SemaphoreType.DMA((2,)), pltpu.SemaphoreType.DMA((32,)),
        pltpu.SemaphoreType.DMA((32,)),
    ]
    outs = pl.pallas_call(
        layer_kernel,
        out_shape=out_shape,
        in_specs=[hbm] * 7 + [vmem] * 8,
        out_specs=(hbm,) * 8,
        scratch_shapes=scratch,
        compiler_params=pltpu.CompilerParams(
            collective_id=0, has_side_effects=True, vmem_limit_bytes=64 * 1024 * 1024 - 65536
        ),
        name="layer",
    )(
        tokens, cotangent, adaptive, mixer, projection, expand, contract,
        condition, row_of(shifts), row_of(prenorm), row_of(postnorm), row_of(offsets), row_of(baseline),
        jnp.asarray(cosine), jnp.asarray(sine),
    )
    layer_output, grad_tokens, ge, gc, gp, gm, vec, _ = outs
    core = lax.rem(lax.axis_index("seq"), 2)
    w = lax.axis_index("wide")

    def by_columns(part):
        out = lax.psum_scatter(part.astype(F32), "wide", scatter_dimension=0, tiled=True)
        out = lax.all_gather(out, "seq", axis=0)
        return out[0:2] + out[2:4]

    def by_rows(part):
        whole_part = jnp.zeros((2 * part.shape[0], part.shape[1]), F32)
        whole_part = lax.dynamic_update_slice(whole_part, part.astype(F32), (core * part.shape[0], 0))
        out = lax.psum_scatter(whole_part, "wide", scatter_dimension=0, tiled=True)
        return lax.psum(out, "seq")

    grad_expand = jnp.concatenate(list(by_columns(ge)), axis=-1)
    mixed = by_columns(gm.reshape(pairs, width, 3, PAIR).transpose(1, 2, 0, 3).reshape(width, 3 * half))
    mixed = mixed.reshape(2, -1, 3, half).transpose(1, 2, 0, 3)
    grad_mixer = mixed.reshape(mixed.shape[0], 3 * width)
    grad_contract = by_rows(gc)
    grad_projection = by_rows(gp)

    every = lax.all_gather(vec, ("wide", "seq"), axis=0)
    every = every.reshape(wide_count, 2, 2, 16, width)
    every = (every[:, :, 0] + every[:, :, 1]).reshape(2 * wide_count, 16, width)
    grad_mod = every[:, :6].reshape(2 * wide_count, 6 * width)
    sums = jnp.sum(every[:, 6:13], axis=0)
    conditions = lax.all_gather(condition, "wide", axis=0, tiled=True)
    silu_all = jax.nn.silu(conditions)
    own_rows = adaptive.shape[0] // wide_count
    highest = lax.Precision.HIGHEST
    grad_adaptive = jnp.dot(
        lax.dynamic_slice_in_dim(silu_all, w * own_rows, own_rows, axis=1).T, grad_mod, precision=highest
    )

    def own(vector):
        size = vector.shape[0] // wide_count
        return lax.dynamic_slice_in_dim(vector, w * size, size)

    here = lax.dynamic_slice_in_dim(grad_mod, w * rows, rows, axis=0)
    _, silu_back = jax.vjp(jax.nn.silu, condition)
    (grad_time,) = silu_back(jnp.dot(here, adaptive.astype(F32).T, precision=highest))
    return (
        layer_output, grad_tokens, grad_time, grad_adaptive, own(jnp.sum(grad_mod, axis=0)), own(sums[0]),
        grad_mixer, grad_projection, own(sums[1]), grad_expand, own(sums[3:7].reshape(-1)), grad_contract,
        own(sums[2]),
    )


def solution(mesh):
    rows = P("wide", "seq", None)
    by_wide = P("wide", None)
    in_specs = (rows, by_wide, rows) + (P(),) * 10
    out_specs = (
        rows, rows, by_wide, by_wide, P("wide"), P("wide"), by_wide, by_wide, P("wide"), by_wide, P("wide"),
        by_wide, P("wide"),
    )
    return jax.shard_map(
        functools.partial(local_part, mesh.shape["wide"]),
        mesh=mesh, in_specs=in_specs, out_specs=out_specs, check_vma=False,
    )
```

time: 1220 us -> 616 us (0.50)
  waiting for transfers between devices: 705 us -> 417 us
  matrix products: 263 us -> 2.83 us
  Pallas kernels: 0 us -> 119 us
  local copies, waits for them, and re-layouts: 129 us -> 31.8 us
  other arithmetic: 47.9 us -> 11.4 us
  blocking collectives: 43.9 us -> 15.9 us
    reduce_scatter x7 -> x4, waiting for transfers between devices: 657 us -> 377 us  [the longest x2 201 us: by_rows(): out = lax.psum_scatter(whole_part, 'wide', scatter_dimension=0, tiled=True)]
    dot_general x29 -> x2, matrix products: 263 us -> 2.83 us  [the longest x1 1.59 us: local_part(): jnp.dot(here, adaptive.astype(F32).T, precision=highest)]
    pallas_call x0 -> x1, Pallas kernels: none -> 119 us  [local_part(): pl.pallas_call(layer_kernel, out_shape=out_shape, in_specs=[hbm] * 7 + [v...]
    dynamic_update_slice x10 -> x0, local copies, waits for them, and re-layouts: 30.1 us -> none  [the longest x6 25.9 us: local(): lax.map(attend_backward, (queries, key_again, value_again, log_total, gra...]
    unnamed x1 -> x0, blocking collectives: 30 us -> none
    while x36 -> x0, local copies, waits for them, and re-layouts: 21.4 us -> none  [the longest x3 11.7 us: local(): lax.map(attend_forward, (queries, key_whole, value_whole))]
    all_gather x2 -> x3, waiting for transfers between devices: 20 us -> 0.01 us  [the longest x2 0.01 us: by_columns(): out = lax.all_gather(out, 'seq', axis=0)]
    reduce_sum x11 -> x2, other arithmetic: 19.7 us -> 0.1 us  [the longest x1 0.06 us: local_part(): sums = jnp.sum(every[:, 6:13], axis=0)]
  transfers between devices with their start and end apart: 10 -> 8, of which waited for: 9 -> 5; matrix products, arithmetic and copies ran while one was open for 10% -> 4% of each run, Pallas kernels for 0% -> 0%
where the time goes in v1:
time: 616 us; the launch traced here: 613 us
  waiting for transfers between devices  417 us (68%)
  Pallas kernels  119 us (19%)
  local copies, waits for them, and re-layouts  31.8 us (5%)
  blocking collectives  15.9 us (3%)
  between operations  15.7 us (3%)
  other arithmetic  11.4 us (2%)
    reduce_scatter x2, waiting for transfers between devices, by_rows(): out = lax.psum_scatter(whole_part, 'wide', scatter_dimension=0, tiled=True)  201 us
    reduce_scatter x2, waiting for transfers between devices, by_columns(): lax.psum_scatter(part.astype(F32), 'wide', scatter_dimension=0, tiled=True)  176 us
    pallas_call x1, Pallas kernels, local_part(): pl.pallas_call(layer_kernel, out_shape=out_shape, in_specs=[hbm] * 7 + [v...  119 us
    psum x1, waiting for transfers between devices, by_rows(): return lax.psum(out, 'seq')  38.9 us
    all_gather x1, blocking collectives, local_part(): conditions = lax.all_gather(condition, 'wide', axis=0, tiled=True)  15.9 us
  transfers between devices with their start and end apart: 8, of which 5 were waited for; matrix products, arithmetic and copies ran while one was open for 4% of the time, Pallas kernels for 0%

profile of v1, /device:TPU:1, one launch (start us, length us, event | category | flops | bytes accessed | tf_op | source)
XLA Modules:
  0.0 613.3 jit_solution(14188379392910836323)
XLA Ops:
  8.1 1.3 reshape.70.shifts
  9.4 1.3 reshape.71.prenorm
  10.7 1.3 reshape.72.postnorm
  11.9 1.3 reshape.74.baseline
  13.2 118.7 %layer.1 = (bf16[2,256,768]{2,1,0:T(8,128)(2,1)}, bf16[2,256,768]{2,1,0:T(8,128)(2,1)}, bf16[768,1536]{1,0:T(8,128)(2,1)}, bf16[1536,768]{1,0:T(8,128)(2,1)}, bf...) custom-call(bf16[2,256,768]{2,1,0:T(8,128)(2,1)} %tok_h.1, ...), custom_call_target="tpu_custom_call" | custom-call | tf_op jit(solution)/shard_map/layer/pallas_call | solution.py:499
  132.0 4.3 copy.35
  136.3 2.4 copy.36
  138.6 3.0 copy.39
  141.7 1.6 copy-done.3
  143.3 2.8 convert_element_type.27
  146.7 77.7 %reduce-scatter.13.cloned.1.call-done = f32[96,1152]{1,0:T(8,128)} async-done(((f32[768,1152]{1,0:T(8,128)}), f32[96,1152]{1,0:T(8,128)}) %reduce-scatter.13.cloned.1.call-update) | async-done | bytes 442384 | tf_op jit(solution)/shard_map/reduce_scatter | solution.py:519
  224.5 98.6 %reduce-scatter.9.cloned.1.call-done = f32[96,1536]{1,0:T(8,128)} async-done(((f32[768,1536]{1,0:T(8,128)}), f32[96,1536]{1,0:T(8,128)}) %reduce-scatter.9.cloned.1.call-update) | async-done | bytes 589840 | tf_op jit(solution)/shard_map/reduce_scatter | solution.py:519
  323.4 1.5 copy-done
  325.0 4.2 broadcast_in_dim.7
  329.2 2.5 convert_dynamic-update-slice_fusion
  332.5 15.9 %all-gather.3 = f32[8,2,128]{2,1,0:T(2,128)S(1)} all-gather(f32[1,2,128]{2,1,0:T(2,128)S(1)} %bitcast.32), channel_id=1, replica_groups=mesh['wide'=8,'seq'=4] {'wide'}, dimensions={0}, use_global_device_ids=true | all-gather | bytes 9216 | tf_op jit(solution)/shard_map/all_gather | solution.py:541
  348.4 1.5 slice_add_fusion.2
  353.9 1.6 fusion.13
  355.5 1.5 slice_add_fusion.1
  358.1 1.6 reshape.78
  359.7 1.8 slice_add_fusion
  361.5 33.9 %reduce-scatter.7.cloned.1.call-done = f32[96,768]{1,0:T(8,128)} async-done(((f32[768,768]{1,0:T(8,128)}), f32[96,768]{1,0:T(8,128)}) %reduce-scatter.7.cloned.1.call-update) | async-done | bytes 294928 | tf_op jit(solution)/shard_map/reduce_scatter | solution.py:526
  395.3 166.9 %reduce-scatter.11.cloned.1.call-done = f32[384,768]{1,0:T(8,128)} async-done(((f32[3072,768]{1,0:T(8,128)}), f32[384,768]{1,0:T(8,128)}) %reduce-scatter.11.cloned.1.call-update) | async-done | bytes 1179664 | tf_op jit(solution)/shard_map/reduce_scatter | solution.py:526
  563.5 38.9 %all-reduce.3.cloned.1.call-done = (f32[96,768]{1,0:T(8,128)}, f32[384,768]{1,0:T(8,128)}) async-done(((f32[96,768]{1,0:T(8,128)}, f32[384,768]{1,0:T(8,128)}), (f32[96,768]{1,0:T(8,128)}, f32[384,768]{1,0:T(8,128)})) %all-reduce.3.cloned.1.call-update) | async-done | bytes 1474576 | tf_op jit(solution)/shard_map/psum | solution.py:527
  (59 shorter events, 11.5 us)
Async XLA Ops:
  8.0 216.4 %reduce-scatter.13.cloned.1.call-start = ((), (), s32[]{:S(2)}) async-start(), calls=%async_computation.10 | async-start | bytes 3981312 | tf_op jit(solution)/shard_map/reduce_scatter | solution.py:519
  141.6 1.7 copy-start.3
  141.7 181.4 %reduce-scatter.9.cloned.1.call-start = ((), (), s32[]{:S(2)}) async-start(), calls=%async_computation.5 | async-start | bytes 5308416 | tf_op jit(solution)/shard_map/reduce_scatter | solution.py:519
  146.1 177.2 %copy-start.7 = (bf16[384,768]{1,0:T(8,128)(2,1)S(1)}, bf16[384,768]{1,0:T(8,128)(2,1)}, u32[]{:S(2)}) copy-start(bf16[384,768]{1,0:T(8,128)(2,1)} %get-tuple-element.24) | copy-start | bytes 1769476
  146.1 202.2 %all-gather.8.cloned.1.call-start = ((), (), s32[]{:S(2)}) async-start(), calls=%async_computation.7 | async-start | bytes 1622016 | tf_op jit(solution)/shard_map/all_gather | solution.py:536
  146.7 208.8 %all-gather.10.cloned.1.call-start = ((), (), s32[]{:S(2)}) async-start(), calls=%async_computation.8 | async-start | bytes 2211840 | tf_op jit(solution)/shard_map/all_gather | solution.py:520
  224.4 135.3 %all-gather.12.cloned.1.call-start = ((), (), s32[]{:S(2)}) async-start(), calls=%async_computation.9 | async-start | bytes 2949120 | tf_op jit(solution)/shard_map/all_gather | solution.py:520
  323.1 72.2 %reduce-scatter.7.cloned.1.call-start = ((), (), s32[]{:S(2)}) async-start(), calls=%async_computation.4 | async-start | bytes 2654208 | tf_op jit(solution)/shard_map/reduce_scatter | solution.py:526
  323.4 1.5 copy-start
  325.0 237.3 %reduce-scatter.11.cloned.1.call-start = ((), (), s32[]{:S(2)}) async-start(), calls=%async_computation.6 | async-start | bytes 10616832 | tf_op jit(solution)/shard_map/reduce_scatter | solution.py:526
  325.0 4.2 copy-start.2
  331.8 0.7 copy-start.9
  331.8 270.6 %all-reduce.3.cloned.1.call-start = ((), (), s32[]{:S(2)}) async-start(), calls=%async_computation.11 | async-start | bytes 2949120 | tf_op jit(solution)/shard_map/psum | solution.py:527
  349.9 4.0 copy-start.1
  562.4 40.1 %copy-start.6 = (bf16[2,256,768]{2,1,0:T(8,128)(2,1)S(1)}, bf16[2,256,768]{2,1,0:T(8,128)(2,1)}, u32[]{:S(2)}) copy-start(bf16[2,256,768]{2,1,0:T(8,128)(2,1)} %get-tuple-element.51) | copy-start | bytes 2359300
  562.4 40.9 %copy-start.5 = (bf16[2,256,768]{2,1,0:T(8,128)(2,1)S(1)}, bf16[2,256,768]{2,1,0:T(8,128)(2,1)}, u32[]{:S(2)}) copy-start(bf16[2,256,768]{2,1,0:T(8,128)(2,1)} %get-tuple-element.52) | copy-start | bytes 2359300
  602.4 1.8 copy-start.8
  602.4 2.5 copy-start.4
Sparse Core Ops, SparseCore 0:
  141.8 82.5 reduce-scatter.12
  228.1 94.9 reduce-scatter.8
  327.4 67.8 reduce-scatter.6
  398.8 163.4 reduce-scatter.10
Sparse Core Ops, SparseCore 1:
  149.5 67.4 all-gather.7
  224.5 20.5 all-gather.9
  323.2 24.1 all-gather.11
  562.4 40.0 all-reduce.2

commit v2 on v1

v2 whole, which is shorter than its diff:
```python
import functools
import itertools
import math
import types

import jax
import jax.numpy as jnp
import numpy as np
from jax import lax
from jax.experimental import pallas as pl
from jax.experimental.pallas import tpu as pltpu
from jax.sharding import PartitionSpec as P

F32 = jnp.float32
BF16 = jnp.bfloat16
MESH = pl.DeviceIdType.MESH
HDIM = 64
PAIR = 2 * HDIM
EPSILON = 1e-06
GELU_A = 0.7978845608
GELU_B = 0.044715

ROWS_BY_ROWS = (((1,), (1,)), ((), ()))
COLS_BY_COLS = (((0,), (0,)), ((), ()))


def dot(a, b, dims=None):
    if dims is None:
        return jnp.dot(a, b, preferred_element_type=F32)
    return lax.dot_general(a, b, dims, preferred_element_type=F32)


def normalize(values):
    center = values - jnp.mean(values, axis=-1, keepdims=True)
    scale = lax.rsqrt(jnp.mean(center * center, axis=-1, keepdims=True) + EPSILON)
    return center * scale, scale


def normalize_back(grad, normal, scale):
    first = jnp.mean(grad, axis=-1, keepdims=True)
    second = jnp.mean(grad * normal, axis=-1, keepdims=True)
    return scale * (grad - first - normal * second)


def turn(values):
    lane = lax.broadcasted_iota(jnp.int32, values.shape, 1)
    first = lax.rem(lane, HDIM) < HDIM // 2
    return jnp.where(
        first, pltpu.roll(values, PAIR - HDIM // 2, 1), pltpu.roll(values, HDIM // 2, 1)
    )


def column_sum(values):
    return jnp.sum(values, axis=0, keepdims=True)


def kernel_buffers(span, width, extent, ff):
    total = 4 * span
    half = width // 2
    pairs = half // PAIR
    uf = ff // 2
    ub = uf // 2
    strip = width // 16
    block = ff // 16
    V = pltpu.VMEM
    piece = (2, span, width)
    whole = (total, width)
    two = lambda n: (2,) * n
    wide_strip = (strip, width)
    half_strip = (strip, half)
    tall = (block, half)
    return dict(
        tok=V(piece, BF16), cot=V(piece, BF16), adap=V((extent, 6 * width), BF16),
        mix=V((width, 3 * half), BF16), proj=V((width, width), BF16), exp=V((width, uf), BF16),
        con=V((uf, width), BF16), mod=V((8, width), F32),
        hid_a=V(whole, BF16), qq=V((pairs, total, PAIR), BF16), kk=V((pairs, total, PAIR), BF16),
        vv=V((pairs, total, PAIR), BF16), q_t=V((half, total), BF16),
        est=V((2, span, total), BF16), inv_l=V((total, PAIR), F32),
        att_s=V((pairs, total, PAIR), BF16), att=V(piece, BF16),
        branch=V(piece, BF16), middle=V(piece, F32), hid_f=V(whole, BF16), gnar=V(whole, BF16),
        gbr=V(whole, BF16), act=V((total, ub), BF16), gwid=V((total, ub), BF16),
        nacc=V(whole, F32), hacc=V(whole, F32), nsend=V(piece, BF16),
        hsend=V(piece, BF16), hrecv=V(piece, BF16),
        dom=V((total, PAIR), BF16), dom_t=V((PAIR, total), BF16), dsum=V((total, PAIR), F32),
        dv_t=V((PAIR, total), F32), dk_t=V((PAIR, total), F32), dq=V((total, PAIR), F32),
        ge=V((2,) + two(4) + wide_strip, BF16), gc=V(two(4) + tall, BF16), gcs=V(two(2) + tall, BF16),
        gp=V(two(4) + half_strip, BF16), gps=V(two(3) + half_strip, BF16),
        e1=V((2,) + two(3) + wide_strip, BF16), e2=V((2,) + two(2) + wide_strip, BF16),
        e3=V((2,) + two(1) + wide_strip, BF16), e4=V((2,) + wide_strip, BF16),
        c1=V(two(3) + tall, BF16), c2=V(two(2) + tall, BF16), c3=V(two(1) + tall, BF16), c4=V(tall, BF16),
        p1=V(two(3) + half_strip, BF16), p2=V(two(2) + half_strip, BF16), p3=V(two(1) + half_strip, BF16),
        p4=V(half_strip, BF16),
        m1=V((pairs, 8 * strip, half), BF16), m2=V((pairs, 4 * strip, half), BF16),
        m3=V((pairs, 2 * strip, half), BF16), m4=V((pairs,) + half_strip, BF16),
        ag_e=V(two(3) + wide_strip, BF16), ag_c=V(two(2) + tall, BF16),
        ag_m=V(two(2) + (pairs + 1,) + half_strip, BF16),
        va=V((2, 16, half), F32), vb=V((2, 8, half), F32), va_r=V((16, half), F32), vb_r=V((8, half), F32),
        all_a=V((2, 16, 16, half), F32), all_b=V((2, 16, 8, half), F32), st=V((extent, 16), F32),
        lsem=pltpu.SemaphoreType.DMA((64,)), esem=pltpu.SemaphoreType.DMA((2,)),
        ssem=pltpu.SemaphoreType.DMA((100,)), rsem=pltpu.SemaphoreType.DMA((100,)),
    )


INPUTS = (
    "tok_h", "cot_h", "adap_h", "mix_h", "proj_h", "exp_h", "con_h",
    "cond", "shifts", "prenorm", "postnorm", "offsets", "baseline", "cosine", "sine",
)
GRADS = ("out_h", "gtok_h", "oe_h", "oc_h", "op_h", "om_h", "e_h")
FINALS = ("time_o", "adaptive_o", "shifts_o", "prenorm_o", "postnorm_o", "offsets_o", "baseline_o")
PARTIALS = ("all_a_h", "all_b_h")


def layer_kernel(leftover, names, *refs):
    R = types.SimpleNamespace(**dict(zip(names, refs)))
    R.nrecv = R.att
    span = R.tok.shape[1]
    width = R.tok.shape[2]
    total = R.hid_a.shape[0]
    half = width // 2
    pairs = half // PAIR
    blocks = total // span
    ub = R.exp.shape[1] // 2
    strip = width // 16
    block = ub // 4
    w = lax.axis_index("wide")
    s = lax.axis_index("seq")
    y = lax.div(s, 2)
    c = lax.rem(s, 2)
    hi = lax.div(w, leftover)
    b0 = lax.rem(hi, 2)
    b1 = lax.rem(lax.div(hi, 2), 2)
    b2 = lax.div(hi, 4)
    core_dev = (w, y * 2 + 1 - c)
    y_dev = (w, (1 - y) * 2 + c)
    dev0 = (w + leftover * (1 - 2 * b0), s)
    dev1 = (w + 2 * leftover * (1 - 2 * b1), s)
    dev2 = (w + 4 * leftover * (1 - 2 * b2), s)
    remote_count = itertools.count()
    local_count = itertools.count()
    sent = []

    def rows_of(p):
        return pl.ds(pl.multiple_of(p * span, span), span)

    def remote(src, dst, k, dev):
        return pltpu.make_async_remote_copy(
            src_ref=src, dst_ref=dst, send_sem=R.ssem.at[k], recv_sem=R.rsem.at[k],
            device_id=dev, device_id_type=MESH,
        )

    class Link:
        def __init__(self, item):
            self.item, self.open = item, False
            sent.append(self)

        def start(self):
            self.item.start()
            self.open = True

        def wait_recv(self):
            self.item.wait_recv()

        def wait_send(self):
            self.item.wait_send()
            self.open = False

    def link(src, dst, dev):
        return Link(remote(src, dst, next(remote_count), dev))

    def local(src, dst):
        return pltpu.make_async_copy(src, dst, R.lsem.at[next(local_count)])

    own_place = [rows_of(2 * j + c) for j in range(2)]
    other_place = [rows_of(2 * j + 1 - c) for j in range(2)]

    adap_load = local(R.adap_h, R.adap)
    tok_load = local(R.tok_h.at[y], R.tok.at[y])
    cot_load = local(R.cot_h.at[y], R.cot.at[y])
    mix_loads = []
    for j in range(pairs):
        for b in range(3):
            mix_loads.append(local(
                R.mix_h.at[:, pl.ds(pl.multiple_of(b * width + c * half + j * PAIR, PAIR), PAIR)],
                R.mix.at[:, pl.ds((j * 3 + b) * PAIR, PAIR)],
            ))
    proj_load = local(R.proj_h, R.proj)
    exp_load = local(R.exp_h.at[:, pl.ds(pl.multiple_of(c * 2 * ub, PAIR), 2 * ub)], R.exp)
    con_load = local(R.con_h.at[pl.ds(pl.multiple_of(c * 2 * ub, PAIR), 2 * ub), :], R.con)
    for item in [adap_load, tok_load, cot_load] + mix_loads + [proj_load, exp_load, con_load]:
        item.start()

    barrier = pltpu.get_barrier_semaphore()
    for dev in (core_dev, y_dev, dev0, dev1, dev2):
        pl.semaphore_signal(barrier, inc=1, device_id=dev, device_id_type=MESH)
    pl.semaphore_wait(barrier, 5)

    tok_swap = link(R.tok_h.at[1 - y], R.tok.at[y], y_dev)
    cot_swap = link(R.cot_h.at[1 - y], R.cot.at[y], y_dev)
    hid_a_push = []
    for j in (y, 1 - y):
        place = rows_of(2 * j + c)
        hid_a_push.append(link(R.hid_a.at[place, :], R.hid_a.at[place, :], core_dev))
    gnar_base = next(remote_count)
    next(remote_count)
    gnar_push = [Link(remote(R.gnar.at[p, :], R.gnar.at[p, :], gnar_base + j, core_dev)) for j, p in enumerate(own_place)]
    hid_f_base = next(remote_count)
    next(remote_count)
    hid_f_push = [Link(remote(R.hid_f.at[p, :], R.hid_f.at[p, :], hid_f_base + j, core_dev)) for j, p in enumerate(own_place)]
    att_base = next(remote_count)
    for _ in range(2 * pairs - 1):
        next(remote_count)
    hsum_base = next(remote_count)
    next(remote_count)
    nsum_base = next(remote_count)
    next(remote_count)
    hsum_push = [Link(remote(R.hsend.at[j], R.hrecv.at[j], hsum_base + j, core_dev)) for j in range(2)]
    nsum_push = [Link(remote(R.nsend.at[j], R.nrecv.at[j], nsum_base + j, core_dev)) for j in range(2)]
    gbr_push = [link(R.gbr.at[p, :], R.gbr.at[p, :], core_dev) for p in own_place]
    asum_push = [link(R.hsend.at[j], R.hrecv.at[j], core_dev) for j in range(2)]
    def stage(n, j):
        return R.gwid.at[pl.ds(pl.multiple_of((2 * n + j) * span, span), span), :]

    out_push = link(stage(0, 1 - y), R.out_h.at[y], y_dev)
    gtok_push = link(stage(1, 1 - y), R.gtok_h.at[y], y_dev)

    class Halving:
        def __init__(self, acc, steps):
            self.acc = acc
            self.steps = []
            place = ()
            for bit, dev, recv in steps:
                self.steps.append((link(acc.at[place + (1 - bit,)], recv, dev), place + (bit,), recv))
                place = place + (bit,)

        def send(self, t):
            self.steps[t][0].start()

        def land(self, t, into=None):
            item, place, recv = self.steps[t]
            item.wait_recv()
            value = self.acc.at[place][...] + recv[...]
            if into is None:
                self.acc.at[place][...] = value
            else:
                into[...] = value

    class Strips:
        def __init__(self, ref, lanes):
            self.ref, self.lanes = ref, lanes

        @property
        def at(self):
            return self

        def __getitem__(self, bits):
            start = 0
            for n, bit in enumerate(bits):
                start = start + bit * (8 >> n)
            rows = (16 >> len(bits)) * strip
            return self.ref.at[pl.ds(pl.multiple_of(start * strip, strip), rows), self.lanes]

    x_step, z_step, y_step, q_step = (b0, dev0), (b1, dev1), (y, y_dev), (b2, dev2)
    sum_e = [
        Halving(R.ge.at[i], [z_step + (R.e1.at[i],), y_step + (R.e2.at[i],), x_step + (R.e3.at[i],), q_step + (R.e4.at[i],)])
        for i in range(2)
    ]
    sum_m = [
        Halving(Strips(R.exp, pl.ds(j * half, half)), [x_step + (R.m1.at[j],), z_step + (R.m2.at[j],), y_step + (R.m3.at[j],), q_step + (R.m4.at[j],)])
        for j in range(pairs)
    ]
    swap_p = link(R.gps, R.gp.at[:, :, :, c], core_dev)
    sum_p = Halving(R.gp, [y_step + (R.p1,), x_step + (R.p2,), z_step + (R.p3,), q_step + (R.p4,)])
    swap_c = [link(R.gcs, R.gc.at[:, :, i, c], core_dev) for i in range(2)]
    first_c = [link(R.gc.at[1 - b0, :, i], R.c1.at[i], dev0) for i in range(2)]
    second_c = [link(R.gc.at[b0, 1 - y, i], R.c2.at[i], y_dev) for i in range(2)]
    third_c = link(R.gc.at[b0, y, 1 - b1], R.c3, dev1)
    fourth_c = link(R.gc.at[b0, y, b1, 1 - b2], R.c4, dev2)

    def land_c1(i):
        first_c[i].wait_recv()
        R.gc[b0, :, i] = R.gc[b0, :, i] + R.c1[i]

    def land_c2(i):
        second_c[i].wait_recv()
        R.gc[b0, y, i] = R.gc[b0, y, i] + R.c2[i]

    def land_c3():
        third_c.wait_recv()
        R.gc[b0, y, b1] = R.gc[b0, y, b1] + R.c3[...]

    def land_c4():
        fourth_c.wait_recv()
        R.ag_c[c, y] = R.gc[b0, y, b1, b2] + R.c4[...]

    y_e, core_e = link(R.ag_e.at[c, y], R.ag_e.at[c, y], y_dev), link(R.ag_e.at[c], R.ag_e.at[c], core_dev)
    y_c, core_c = link(R.ag_c.at[c, y], R.ag_c.at[c, y], y_dev), link(R.ag_c.at[c], R.ag_c.at[c], core_dev)
    most, last = pl.ds(0, pairs), pl.ds(pairs, 1)
    y_m, core_m = [], []
    for part in (most, last):
        y_m.append(link(R.ag_m.at[c, y, part], R.ag_m.at[c, y, part], y_dev))
        core_m.append(link(R.ag_m.at[c, :, part], R.ag_m.at[c, :, part], core_dev))

    def add_row(ref, r, value):
        for n in range(2):
            ref[n, pl.ds(r, 1), :] += value[:, n * half : (n + 1) * half]

    chip = y * 8 + hi

    class Gather:
        def __init__(self, part, recv, every):
            self.part, self.recv, self.every = part, recv, every
            self.first = link(part.at[1 - c], recv, core_dev)
            self.steps = []
            for t, dev in enumerate((dev0, dev1, dev2, y_dev)):
                size = 2**t
                start = lax.div(chip, size) * size
                ref = every.at[c, pl.ds(start, size)]
                self.steps.append(link(ref, ref, dev))
            self.steps.append(link(every.at[c], every.at[c], core_dev))

        def start(self):
            self.first.start()

        def step(self, t):
            if t == 0:
                self.first.wait_recv()
                self.every[c, chip] = self.part[c] + self.recv[...]
            else:
                self.steps[t - 1].wait_recv()
            self.steps[t].start()

        def finish(self):
            self.steps[-1].wait_recv()

    gather_a = Gather(R.va, R.va_r, R.all_a)
    gather_b = Gather(R.vb, R.vb_r, R.all_b)

    tok_swap.start()
    cot_swap.start()
    R.va[...] = jnp.zeros_like(R.va)
    R.vb[...] = jnp.zeros_like(R.vb)

    adap_load.wait()
    crow = jnp.where(y == 0, R.cond[0:1, :], R.cond[1:2, :])
    crow = crow * (1.0 / (1.0 + jnp.exp(-crow)))
    extent = crow.shape[1]
    R.va[0, 10:11, :extent] = crow * (1 - c).astype(F32)
    eye = lax.broadcasted_iota(jnp.int32, (extent, extent), 0) == lax.broadcasted_iota(
        jnp.int32, (extent, extent), 1
    )
    ccol = jnp.sum(jnp.where(eye, jnp.broadcast_to(crow, (extent, extent)), 0.0), axis=1, keepdims=True)
    shifts = R.shifts[...].reshape(1, 6 * width)
    for n in range(6):
        part = pl.ds(n * width, width)
        R.mod[n : n + 1, :] = column_sum(R.adap[:, part].astype(F32) * ccol) + shifts[:, n * width : (n + 1) * width]
    pregain = R.prenorm[...].reshape(1, width)
    postgain = R.postnorm[...].reshape(1, width)

    def first_norm(j, t):
        normal, _ = normalize(R.tok[j].astype(F32))
        value = normal * (pregain * (1.0 + R.mod[1:2, :])) + R.mod[0:1, :]
        R.hid_a[rows_of(2 * j + c), :] = value.astype(BF16)
        hid_a_push[t].start()

    def project(p):
        place = rows_of(p)
        mixed = dot(R.hid_a[place, :], R.mix[...])
        cos_here = R.cosine[place, :]
        sin_here = R.sine[place, :]
        for j in range(pairs):
            base = j * 3 * PAIR
            query = mixed[:, base : base + PAIR]
            query = (query * cos_here + turn(query) * sin_here).astype(BF16) * jnp.asarray(
                HDIM ** (-0.5), BF16
            )
            R.qq[j, place, :] = query
            key = mixed[:, base + PAIR : base + 2 * PAIR]
            R.kk[j, place, :] = (key * cos_here + turn(key) * sin_here).astype(BF16)
            R.vv[j, place, :] = mixed[:, base + 2 * PAIR : base + 3 * PAIR].astype(BF16)

    tok_load.wait()
    first_norm(y, 0)
    for item in mix_loads:
        item.wait()
    project(2 * y + c)
    tok_swap.wait_recv()
    first_norm(1 - y, 1)
    hid_a_push[0].wait_recv()
    project(2 * y + 1 - c)
    project(2 * (1 - y) + c)
    hid_a_push[1].wait_recv()
    project(2 * (1 - y) + 1 - c)
    for j in range(pairs):
        R.q_t[j * PAIR : (j + 1) * PAIR, :] = R.qq[j].T

    cot_load.wait()
    cot_swap.wait_recv()
    for j in range(2):
        low = (R.cot[j].astype(F32) * R.mod[5:6, :]).astype(BF16)
        R.gnar[own_place[j], :] = low
        add_row(R.va, 5, column_sum(low.astype(F32)))
        gnar_push[j].start()

    def e_copy(n, slot):
        return pltpu.make_async_copy(R.est.at[slot], R.e_h.at[n], R.esem.at[slot])

    def att_push(j, jj):
        lanes = pl.ds(pl.multiple_of(c * half + j * PAIR, PAIR), PAIR)
        return remote(
            R.att_s.at[j, other_place[jj], :], R.att.at[jj, :, lanes], att_base + 2 * j + jj, core_dev
        )

    lane_pair = lax.broadcasted_iota(jnp.int32, (span, PAIR), 1)
    lane_long = lax.broadcasted_iota(jnp.int32, (total, PAIR), 1)

    def in_head(lane, hh):
        return lane < HDIM if hh == 0 else lane >= HDIM

    def attend(j, carry):
        def score_of(hh, qb):
            query = R.qq[j, qb * span : (qb + 1) * span, :]
            query = jnp.where(in_head(lane_pair, hh), query, jnp.zeros_like(query))
            return dot(query, R.kk[j], ROWS_BY_ROWS)

        values = []
        for hh in range(2):
            there = R.vv[j]
            values.append(jnp.where(in_head(lane_long, hh), there, jnp.ones_like(there)))
        steps = [(hh, qb) for hh in range(2) for qb in range(blocks)]
        score = score_of(*steps[0])
        for index, (hh, qb) in enumerate(steps):
            following = score_of(*steps[index + 1]) if index + 1 < len(steps) else None
            n = j * (2 * blocks) + index
            slot = index % 2
            place = slice(qb * span, (qb + 1) * span)
            top = jnp.max(score, axis=1, keepdims=True)
            low = jnp.exp(score - top).astype(BF16)
            if index < 2:
                @pl.when(j > 0)
                def _():
                    e_copy(n, slot).wait()
            else:
                e_copy(n, slot).wait()
            R.est[slot] = low
            e_copy(n, slot).start()
            grown = dot(low, values[hh])
            inverse = 1.0 / pltpu.roll(grown, HDIM, 1)
            grown = (grown * inverse).astype(BF16)
            head_lane = 0 if hh == 0 else HDIM
            R.inv_l[place, :] = jnp.where(
                lane_pair == 2 * j + hh, inverse[:, head_lane : head_lane + 1], R.inv_l[place, :]
            )
            if hh == 0:
                R.att_s[j, place, :] = grown
            else:
                R.att_s[j, place, :] = jnp.where(lane_pair < HDIM, R.att_s[j, place, :], grown)
            score = following
        lanes = pl.ds(pl.multiple_of(c * half + j * PAIR, PAIR), PAIR)
        for jj in range(2):
            att_push(j, jj).start()
            R.att[jj, :, lanes] = R.att_s[j, own_place[jj], :]
        return carry

    R.inv_l[...] = jnp.zeros_like(R.inv_l)
    lax.fori_loop(0, pairs, attend, 0)
    for slot in range(2):
        e_copy(0, slot).wait()
    for j in range(pairs):
        for jj in range(2):
            att_push(j, jj).wait_recv()

    proj_load.wait()
    for j in range(2):
        grown = dot(R.att[j], R.proj[...])
        R.branch[j] = grown.astype(BF16)
        value = R.tok[j].astype(F32) + R.mod[2:3, :] * grown
        R.middle[j] = value
        normal, _ = normalize(value)
        R.hid_f[own_place[j], :] = (normal * (postgain * (1.0 + R.mod[4:5, :])) + R.mod[3:4, :]).astype(BF16)
        hid_f_push[j].start()

    exp_load.wait()
    con_load.wait()
    offsets = R.offsets[...].reshape(1, 4 * ub)
    offsets = jnp.where(c == 0, offsets[:, : 2 * ub], offsets[:, 2 * ub :])
    for i in range(2):
        units = pl.ds(i * ub, ub)

        def feed(t, carry, i=i, units=units):
            late = lax.div(t, 2)
            j = lax.rem(t, 2)
            place = rows_of(2 * j + lax.rem(c + late + i, 2))
            if i == 0:
                @pl.when(late == 1)
                def _():
                    remote(R.hid_f.at[place, :], R.hid_f.at[place, :], hid_f_base + j, core_dev).wait_recv()
                    remote(R.gnar.at[place, :], R.gnar.at[place, :], gnar_base + j, core_dev).wait_recv()
            else:
                @pl.when(t == 1)
                def _():
                    swap_c[0].wait_recv()
                    first_c[0].start()
            v = dot(R.hid_f[place, :], R.exp[:, units]) + offsets[:, i * ub : (i + 1) * ub]
            square = v * v
            th = jnp.tanh(v * (GELU_A + (GELU_A * GELU_B) * square))
            up = 0.5 + 0.5 * th
            low = (v * up).astype(BF16)
            R.act[place, :] = low
            slope = up + (v * (0.5 - 0.5 * th * th)) * (GELU_A + (3.0 * GELU_A * GELU_B) * square)
            grad = (dot(R.gnar[place, :], R.con[units, :], ROWS_BY_ROWS) * slope).astype(BF16)
            R.gwid[place, :] = grad
            add_row(R.va, 6 + 2 * c + i, column_sum(grad.astype(F32)))
            n_part = dot(low, R.con[units, :])
            h_part = dot(grad, R.exp[:, units], ROWS_BY_ROWS)
            if i == 0:
                R.nacc[place, :] = n_part
                R.hacc[place, :] = h_part
            else:
                R.nacc[place, :] += n_part
                R.hacc[place, :] += h_part

                @pl.when(late == 0)
                def _():
                    R.hsend[j] = R.hacc[place, :].astype(BF16)
                    remote(R.hsend.at[j], R.hrecv.at[j], hsum_base + j, core_dev).start()
                    R.nsend[j] = R.nacc[place, :].astype(BF16)
                    remote(R.nsend.at[j], R.nrecv.at[j], nsum_base + j, core_dev).start()
            return carry

        lax.fori_loop(0, 4, feed, 0)
        if i == 1:
            for item in hsum_push + nsum_push:
                item.open = True
        value = dot(R.hid_f[...], R.gwid[...], COLS_BY_COLS).astype(BF16)
        for n in range(16):
            a2, a1, a0, ay = n // 8, n // 4 % 2, n // 2 % 2, n % 2
            R.ge[i, a1, ay, a0, a2] = value[n * strip : (n + 1) * strip]
        sum_e[i].send(0)
        value = dot(R.act[...], R.gnar[...], COLS_BY_COLS).astype(BF16)
        left, right = value[:, :half], value[:, half:]
        mine = jnp.where(c == 0, left, right)
        theirs = jnp.where(c == 0, right, left)
        if i == 1:
            swap_c[0].wait_send()
        for n in range(4):
            a0, ay = n // 2, n % 2
            R.gcs[a0, ay] = theirs[n * block : (n + 1) * block]
            R.gc[a0, ay, i, c] = mine[n * block : (n + 1) * block]
        swap_c[i].start()

    base_row = R.baseline[...].reshape(1, width)
    for j in range(2):
        place = own_place[j]
        hsum_push[j].wait_recv()
        got = R.hacc[place, :] + R.hrecv[j].astype(F32)
        normal, scale = normalize(R.middle[j])
        add_row(R.va, 1, column_sum(got))
        both = column_sum(got * normal)
        add_row(R.va, 2, both * postgain)
        add_row(R.va, 4, both * (1.0 + R.mod[4:5, :]))
        g = R.cot[j].astype(F32)
        nsum_push[j].wait_recv()
        narrowed = R.nacc[place, :] + R.nrecv[j].astype(F32) + base_row
        R.gwid[j * span : (j + 1) * span, :] = (R.middle[j] + R.mod[5:6, :] * narrowed).astype(BF16)
        add_row(R.va, 3, column_sum(g * narrowed))
        value = g + normalize_back(got * (postgain * (1.0 + R.mod[4:5, :])), normal, scale)
        R.middle[j] = value
        add_row(R.va, 0, column_sum(value * R.branch[j].astype(F32)))
        R.gbr[place, :] = (R.mod[2:3, :] * value).astype(BF16)
        gbr_push[j].start()
        if j == 0:
            swap_c[1].wait_recv()
            first_c[1].start()

    out_local = local(stage(0, y), R.out_h.at[y])
    out_local.start()
    out_push.start()
    gather_a.start()
    for j in range(2):
        gbr_push[j].wait_recv()

    def e_back(n, slot):
        return pltpu.make_async_copy(R.e_h.at[n], R.est.at[slot], R.esem.at[slot])

    e_back(0, 0).start()
    value = jnp.concatenate(
        [dot(R.att_s[j], R.gbr[...], COLS_BY_COLS).astype(BF16) for j in range(pairs)], axis=0
    )
    left, right = value[:, :half], value[:, half:]
    mine = jnp.where(c == 0, left, right)
    theirs = jnp.where(c == 0, right, left)
    for n in range(8):
        a1, a0, ay = n // 4, n // 2 % 2, n % 2
        R.gps[ay, a0, a1] = theirs[n * strip : (n + 1) * strip]
        R.gp[ay, a0, a1, c] = mine[n * strip : (n + 1) * strip]
    swap_p.start()
    sum_e[0].land(0)
    sum_e[0].send(1)

    def m_first(j):
        return lambda: sum_m[j].send(0)

    def forward(item, t, into=None):
        def run():
            item.land(t, into)
            if into is None:
                item.send(t + 1)
        return run

    def c_second(i):
        def run():
            land_c1(i)
            second_c[i].start()
        return run

    def c_third():
        land_c2(0)
        land_c2(1)
        third_c.start()

    def c_fourth():
        land_c3()
        fourth_c.start()

    def c_last():
        land_c4()
        y_c.start()

    def c_core():
        y_c.wait_recv()
        core_c.start()

    def e_y():
        y_e.start()

    def e_core():
        y_e.wait_recv()
        core_e.start()

    def p_first():
        swap_p.wait_recv()
        sum_p.send(0)

    final_e = [R.ag_e.at[c, y, i] for i in range(2)]
    final_m = [R.ag_m.at[c, y, 1 + j] for j in range(pairs)]
    final_p = R.ag_m.at[c, y, 0]
    schedule = {
        (0, 0): [p_first, lambda: gather_a.step(0)],
        (0, 1): [c_second(0), lambda: gather_a.step(1)],
        (0, 2): [m_first(0), forward(sum_e[0], 1)],
        (1, 0): [forward(sum_e[1], 0), lambda: gather_a.step(2)],
        (1, 1): [c_second(1), forward(sum_p, 0), lambda: gather_a.step(3)],
        (1, 2): [m_first(1), forward(sum_e[0], 2)],
        (2, 0): [forward(sum_e[1], 1), forward(sum_m[0], 0), forward(sum_p, 1), lambda: gather_a.step(4)],
        (2, 1): [c_third, forward(sum_e[0], 3, final_e[0]), forward(sum_p, 2)],
        (2, 2): [m_first(2), forward(sum_e[1], 2), forward(sum_m[0], 1), forward(sum_m[1], 0)],
    }

    def service(j, point):
        for k in range(pairs):
            tasks = schedule.get((k, point), [])
            if tasks:
                @pl.when(j == k)
                def _(tasks=tasks):
                    for task in tasks:
                        task()

    own_proj = R.proj[pl.ds(pl.multiple_of(c * half, PAIR), half), :]
    grown = dot(R.gbr[...], own_proj, ROWS_BY_ROWS).astype(BF16)
    for j in range(pairs):
        R.act[:, half + j * PAIR : half + (j + 1) * PAIR] = grown[:, j * PAIR : (j + 1) * PAIR]

    def attend_back(j, carry):
        grown = R.act[:, pl.ds(pl.multiple_of(half + j * PAIR, PAIR), PAIR)].astype(F32)
        product = grown * R.att_s[j].astype(F32)
        table = R.inv_l[...]
        inverse, inner = [], []
        for hh in range(2):
            inverse.append(jnp.sum(jnp.where(lane_long == 2 * j + hh, table, 0.0), axis=1, keepdims=True))
            inner.append(jnp.sum(jnp.where(in_head(lane_long, hh), product, 0.0), axis=1, keepdims=True))
        inverse = jnp.where(in_head(lane_long, 0), inverse[0], inverse[1])
        R.dsum[...] = jnp.where(in_head(lane_long, 0), inner[0], inner[1]) * inverse
        grown = (grown * inverse).astype(BF16)
        R.dom[...] = grown
        R.dom_t[...] = grown.T

        def grad_of(hh, qb):
            there = R.dom[qb * span : (qb + 1) * span, :]
            there = jnp.where(in_head(lane_pair, hh), there, jnp.zeros_like(there))
            return dot(there, R.vv[j], ROWS_BY_ROWS)

        steps = [(hh, qb) for hh in range(2) for qb in range(blocks)]
        grad = grad_of(*steps[0])
        for index, (hh, qb) in enumerate(steps):
            following = grad_of(*steps[index + 1]) if index + 1 < len(steps) else None
            n = j * (2 * blocks) + index
            slot = index % 2
            e_back(n, slot).wait()
            if index + 1 == len(steps):
                @pl.when(j < pairs - 1)
                def _():
                    e_back(n + 1, 1 - slot).start()
            else:
                e_back(n + 1, 1 - slot).start()
            place = slice(qb * span, (qb + 1) * span)
            rows = slice(hh * HDIM, (hh + 1) * HDIM)
            low = R.est[slot]
            grad = (low.astype(F32) * (grad - R.dsum[place, hh * HDIM : hh * HDIM + 1])).astype(BF16)
            q_part = dot(grad, R.kk[j])
            v_part = dot(R.dom_t[rows, place], low)
            k_part = dot(R.q_t[pl.ds(pl.multiple_of(j * PAIR + hh * HDIM, HDIM), HDIM), place], grad)
            if hh == 0:
                R.dq[place, :] = q_part
            else:
                R.dq[place, :] = jnp.where(lane_pair < HDIM, R.dq[place, :], q_part)
            if qb == 0:
                R.dv_t[rows, :] = v_part
                R.dk_t[rows, :] = k_part
            else:
                R.dv_t[rows, :] += v_part
                R.dk_t[rows, :] += k_part
            if qb == blocks - 1:
                service(j, hh)
            grad = following
        gq = R.dq[...] * HDIM ** (-0.5)
        gk = R.dk_t[...].T
        gmx = R.act.at[:, pl.ds(0, 3 * PAIR)]
        gmx[:, :PAIR] = (gq * R.cosine[...] - turn(gq) * R.sine[...]).astype(BF16)
        gmx[:, PAIR : 2 * PAIR] = (gk * R.cosine[...] - turn(gk) * R.sine[...]).astype(BF16)
        gmx[:, 2 * PAIR :] = R.dv_t[...].astype(BF16).T
        value = dot(R.hid_a[...], gmx[...], COLS_BY_COLS).astype(BF16)
        for n in range(16):
            a2, a1, a0, ay = n // 8, n // 4 % 2, n // 2 % 2, n % 2
            index = ((a0 * 2 + a1) * 2 + ay) * 2 + a2
            R.exp[index * strip : (index + 1) * strip, pl.ds(pl.multiple_of(j * half, PAIR), half)] = value[
                n * strip : (n + 1) * strip
            ]
        service(j, 2)
        lanes = pl.ds(pl.multiple_of(j * 3 * PAIR, PAIR), 3 * PAIR)

        def back(p, inner):
            place = rows_of(p)
            part = dot(gmx[place, :], R.mix[:, lanes], ROWS_BY_ROWS)

            @pl.when(j == 0)
            def _():
                R.hacc[place, :] = part

            @pl.when(j > 0)
            def _():
                R.hacc[place, :] += part

            return inner

        lax.fori_loop(0, blocks, back, 0)
        return carry

    lax.fori_loop(0, pairs, attend_back, 0)
    for j in range(2):
        hsum_push[j].wait_send()
        R.hsend[j] = R.hacc[other_place[j], :].astype(BF16)
        asum_push[j].start()

    forward(sum_p, 3, final_p)()
    c_fourth()
    gtok_local = local(stage(1, y), R.gtok_h.at[y])
    for j, item in ((1 - y, gtok_push), (y, gtok_local)):
        got = R.hacc[rows_of(2 * j + c), :] + 0.0
        if item is gtok_push:
            asum_push[0].wait_recv()
            asum_push[1].wait_recv()
        got = got + R.hrecv[j].astype(F32)
        normal, scale = normalize(R.tok[j].astype(F32))
        add_row(R.vb, 0, column_sum(got))
        both = column_sum(got * normal)
        add_row(R.vb, 1, both * pregain)
        add_row(R.vb, 2, both * (1.0 + R.mod[1:2, :]))
        stage(1, j)[...] = (
            R.middle[j] + normalize_back(got * (pregain * (1.0 + R.mod[1:2, :])), normal, scale)
        ).astype(BF16)
        item.start()
    gather_b.start()
    forward(sum_e[1], 3, final_e[1])()
    e_y()
    forward(sum_m[0], 2)()
    forward(sum_m[1], 1)()
    forward(sum_m[2], 0)()
    gather_b.step(0)
    c_last()
    forward(sum_m[0], 3, final_m[0])()
    forward(sum_m[1], 2)()
    forward(sum_m[2], 1)()
    gather_b.step(1)
    e_core()
    forward(sum_m[1], 3, final_m[1])()
    y_m[0].start()
    forward(sum_m[2], 2)()
    gather_b.step(2)
    c_core()
    forward(sum_m[2], 3, final_m[2])()
    y_m[1].start()
    gather_b.step(3)
    y_m[0].wait_recv()
    core_m[0].start()
    gather_b.step(4)
    y_m[1].wait_recv()
    core_m[1].start()

    stores = []

    def store(src, dst):
        item = local(src, dst)
        item.start()
        stores.append(item)

    core_e.wait_recv()
    for n in range(8):
        cc, yy, i = n // 4, n // 2 % 2, n % 2
        store(
            R.ag_e.at[cc, yy, i],
            R.oe_h.at[pl.ds(yy * strip, strip), pl.ds((2 * cc + i) * width, width)],
        )
    core_c.wait_recv()
    for n in range(4):
        cc, yy = n // 2, n % 2
        store(R.ag_c.at[cc, yy], R.oc_h.at[pl.ds(yy * block, block), pl.ds(cc * half, half)])
    gather_a.finish()
    gather_b.finish()
    if leftover == 1:
        finish_vectors(R, hi, width, half, extent)
    else:
        store(R.all_a, R.all_a_h)
        store(R.all_b, R.all_b_h)
    core_m[0].wait_recv()
    for n in range(4):
        cc, yy = n // 2, n % 2
        store(R.ag_m.at[cc, yy, 0], R.op_h.at[pl.ds(yy * strip, strip), pl.ds(cc * half, half)])
    core_m[1].wait_recv()
    for item in hid_f_push:
        item.open = True
        item.wait_send()
    for n in range(4):
        cc, yy = n // 2, n % 2
        for j in range(pairs):
            value = R.ag_m[cc, yy, 1 + j]
            for b in range(3):
                lane = cc * half + j * PAIR
                row = (2 * b + yy) * strip
                R.hid_f[row : row + strip, lane : lane + PAIR] = value[:, b * PAIR : (b + 1) * PAIR]
    for b in range(3):
        store(R.hid_f.at[pl.ds(2 * b * strip, 2 * strip), :], R.om_h.at[:, pl.ds(b * width, width)])
    for item in stores:
        item.wait()
    out_local.wait()
    out_push.wait_recv()
    gtok_local.wait()
    gtok_push.wait_recv()
    for j in range(pairs):
        for jj in range(2):
            att_push(j, jj).wait_send()
    for item in sent:
        if item.open:
            item.wait_send()


def finish_vectors(R, hi, width, half, extent):
    own = extent // 8
    highest = lax.Precision.HIGHEST
    R.st[...] = R.all_a[0, :, 10, :extent].T
    silu_own = R.st[pl.ds(pl.multiple_of(hi * own, own), own), :]
    sections = ((R.all_b, 0), (R.all_b, 1), (R.all_a, 0), (R.all_a, 1), (R.all_a, 2), (R.all_a, 3))
    sums = []
    back = [jnp.zeros((extent, 1), F32) for _ in range(2)]
    for n, (ref, r) in enumerate(sections):
        for h in range(2):
            grads = ref[h, :, r, :]
            lanes = pl.ds(n * width + h * half, half)
            R.adaptive_o[:, lanes] = jnp.dot(silu_own, grads, precision=highest, preferred_element_type=F32)
            sums.append(column_sum(grads))
            table = R.adap[:, lanes].astype(F32)
            for yy in range(2):
                mine = ref[h, pl.ds(yy * 8 + hi, 1), r, :]
                back[yy] = back[yy] + jnp.sum(table * mine, axis=1, keepdims=True)
    eye = lax.broadcasted_iota(jnp.int32, (extent, extent), 0) == lax.broadcasted_iota(
        jnp.int32, (extent, extent), 1
    )
    for yy in range(2):
        row = column_sum(jnp.where(eye, jnp.broadcast_to(back[yy], (extent, extent)), 0.0))
        cond = R.cond[yy : yy + 1, :]
        gate = 1.0 / (1.0 + jnp.exp(-cond))
        R.time_o[yy : yy + 1, :] = row * (gate * (1.0 + cond * (1.0 - gate)))

    def share(vector, out):
        size = vector.shape[1] // 8
        value = jnp.zeros((1, size), F32)
        for k in range(8):
            value = jnp.where(hi == k, vector[:, k * size : (k + 1) * size], value)
        out[...] = value.reshape(size)

    def total_of(ref, r):
        return jnp.concatenate([column_sum(ref[h, :, r, :]) for h in range(2)], axis=1)

    share(jnp.concatenate(sums, axis=1), R.shifts_o)
    share(total_of(R.all_b, 2), R.prenorm_o)
    share(total_of(R.all_a, 4), R.postnorm_o)
    share(jnp.concatenate([total_of(R.all_a, 6 + n) for n in range(4)], axis=1), R.offsets_o)
    share(total_of(R.all_a, 5), R.baseline_o)


def rotary_constants(length):
    half_dim = HDIM // 2
    frequency = np.exp(np.arange(half_dim, dtype=np.float32) * np.float32(-2.0 * math.log(10000.0) / HDIM))
    angles = np.arange(length, dtype=np.float32)[:, None] * frequency[None, :].astype(np.float32)
    angles = angles.astype(np.float64)
    cosine = np.cos(angles).astype(np.float32)
    sine = np.sin(angles).astype(np.float32)
    cosine = np.concatenate([cosine] * 4, axis=-1)
    sine = np.concatenate([-sine, sine, -sine, sine], axis=-1)
    return cosine, sine


def local_part(wide_count, tokens, condition, cotangent, adaptive, shifts, prenorm, mixer, projection, postnorm,
               expand, offsets, contract, baseline):
    rows, span, width = tokens.shape
    total = 4 * span
    half = width // 2
    pairs = half // PAIR
    ff = expand.shape[1]
    extent = adaptive.shape[0]
    leftover = wide_count // 8
    cosine, sine = rotary_constants(total)
    hbm = pl.BlockSpec(memory_space=pl.ANY)
    vmem = pl.BlockSpec(memory_space=pltpu.VMEM)
    shape = jax.ShapeDtypeStruct
    out_shape = [
        shape(tokens.shape, BF16), shape(tokens.shape, BF16), shape((width // 8, ff), BF16),
        shape((ff // 8, width), BF16), shape((width // 8, width), BF16), shape((width // 8, 3 * width), BF16),
        shape((2 * pairs * 4, span, total), BF16),
    ]
    out_specs = [hbm] * len(out_shape)
    names = INPUTS + GRADS
    if leftover == 1:
        names += FINALS
        out_shape += [
            shape(condition.shape, F32), shape((extent // 8, 6 * width), F32), shape((6 * width // 8,), F32),
            shape((width // 8,), F32), shape((width // 8,), F32), shape((ff // 8,), F32), shape((width // 8,), F32),
        ]
        out_specs += [vmem] * len(FINALS)
    else:
        names += PARTIALS
        out_shape += [shape((2, 16, 16, half), F32), shape((2, 16, 8, half), F32)]
        out_specs += [hbm] * len(PARTIALS)
    buffers = kernel_buffers(span, width, extent, ff)
    names += tuple(buffers)
    outs = pl.pallas_call(
        functools.partial(layer_kernel, leftover, names),
        out_shape=tuple(out_shape),
        in_specs=[hbm] * 7 + [vmem] * 8,
        out_specs=tuple(out_specs),
        scratch_shapes=list(buffers.values()),
        compiler_params=pltpu.CompilerParams(
            collective_id=0, has_side_effects=True, vmem_limit_bytes=64 * 1024 * 1024 - 65536
        ),
        name="layer",
    )(
        tokens, cotangent, adaptive, mixer, projection, expand, contract,
        condition, shifts, prenorm, postnorm, offsets, baseline, jnp.asarray(cosine), jnp.asarray(sine),
    )
    layer_output, grad_tokens = outs[0], outs[1]
    grad_expand, grad_contract, grad_projection, grad_mixer = (part.astype(F32) for part in outs[2:6])
    if leftover == 1:
        grad_time, grad_adaptive, grad_shifts, grad_prenorm, grad_postnorm, grad_offsets, grad_baseline = outs[7:]
        return (
            layer_output, grad_tokens, grad_time, grad_adaptive, grad_shifts, grad_prenorm, grad_mixer,
            grad_projection, grad_postnorm, grad_expand, grad_offsets, grad_contract, grad_baseline,
        )

    w = lax.axis_index("wide")

    def among_groups(part):
        size = part.shape[0]
        whole = jnp.zeros((8 * size,) + part.shape[1:], F32)
        whole = lax.dynamic_update_slice_in_dim(whole, part, lax.div(w, leftover) * size, axis=0)
        return lax.psum_scatter(whole, "wide", scatter_dimension=0, tiled=True)

    grad_expand, grad_contract, grad_projection, grad_mixer = (
        among_groups(part) for part in (grad_expand, grad_contract, grad_projection, grad_mixer)
    )
    all_a, all_b = outs[7], outs[8]
    every = jnp.concatenate([all_b, all_a], axis=2)
    every = every.transpose(1, 2, 0, 3).reshape(2, 8, 24, width)
    every = every.transpose(1, 0, 2, 3)
    mine = lax.dynamic_slice_in_dim(every, lax.div(w, leftover), 1, axis=0)[0]
    every = lax.all_gather(mine, "wide", axis=0, tiled=True)
    sections = [0, 1, 8, 9, 10, 11]
    grad_mod = jnp.concatenate([every[:, r] for r in sections], axis=-1)
    silu_all = every[:, 18, :extent]
    highest = lax.Precision.HIGHEST
    own_rows = extent // wide_count
    grad_adaptive = jnp.dot(
        lax.dynamic_slice_in_dim(silu_all, w * own_rows, own_rows, axis=1).T, grad_mod, precision=highest
    )
    sums = jnp.sum(every, axis=0)

    def own(vector):
        size = vector.shape[0] // wide_count
        return lax.dynamic_slice_in_dim(vector, w * size, size)

    here = lax.dynamic_slice_in_dim(grad_mod, w * rows, rows, axis=0)
    _, silu_back = jax.vjp(jax.nn.silu, condition)
    (grad_time,) = silu_back(jnp.dot(here, adaptive.astype(F32).T, precision=highest))
    return (
        layer_output, grad_tokens, grad_time, grad_adaptive, own(jnp.sum(grad_mod, axis=0)), own(sums[2]),
        grad_mixer, grad_projection, own(sums[12]), grad_expand, own(sums[14:18].reshape(-1)), grad_contract,
        own(sums[13]),
    )


def solution(mesh):
    rows = P("wide", "seq", None)
    by_wide = P("wide", None)
    in_specs = (rows, by_wide, rows) + (P(),) * 10
    out_specs = (
        rows, rows, by_wide, by_wide, P("wide"), P("wide"), by_wide, by_wide, P("wide"), by_wide, P("wide"),
        by_wide, P("wide"),
    )
    return jax.shard_map(
        functools.partial(local_part, mesh.shape["wide"]),
        mesh=mesh, in_specs=in_specs, out_specs=out_specs, check_vma=False,
    )
```

time: 616 us -> 178 us (0.29)
  waiting for transfers between devices: 417 us -> 0 us
  Pallas kernels: 119 us -> 163 us
  local copies, waits for them, and re-layouts: 31.8 us -> 5.78 us
  blocking collectives: 15.9 us -> 0 us
  between operations: 15.7 us -> 0.72 us
    reduce_scatter x4 -> x0, waiting for transfers between devices: 377 us -> none  [the longest x2 201 us: by_rows(): out = lax.psum_scatter(whole_part, 'wide', scatter_dimension=0, tiled=True)]
    pallas_call x1, Pallas kernels: 119 us -> 163 us  [local_part(): pl.pallas_call(functools.partial(layer_kernel, leftover, names), out_shap...]
    psum x1 -> x0, waiting for transfers between devices: 38.9 us -> none  [by_rows(): return lax.psum(out, 'seq')]
    all_gather x1 -> x0, blocking collectives: 15.9 us -> none  [local_part(): conditions = lax.all_gather(condition, 'wide', axis=0, tiled=True)]
    reshape x7 -> x0, local copies, waits for them, and re-layouts: 7.13 us -> none  [the longest x4 5.15 us: local_part(): row_of = lambda v: v.reshape(1, -1)]
    convert_element_type x2 -> x0, local copies, waits for them, and re-layouts: 6.68 us -> none  [by_columns(): part.astype(F32)]
  transfers between devices with their start and end apart: 8 -> 0, of which waited for: 5 -> 0; matrix products, arithmetic and copies ran while one was open for 4% -> 0% of each run, Pallas kernels for 0% -> 0%
where the time goes in v2:
time: 178 us; the launch traced here: 177 us
  Pallas kernels  163 us (92%)
  other arithmetic  7.08 us (4%)
  local copies, waits for them, and re-layouts  5.78 us (3%)
    pallas_call x1, Pallas kernels, local_part(): pl.pallas_call(functools.partial(layer_kernel, leftover, names), out_shap...  163 us
    convert_element_type x4, other arithmetic, local_part(): part.astype(F32)  7.08 us
    unnamed x29, local copies, waits for them, and re-layouts  5.78 us

profile of v2, /device:TPU:1, one launch (start us, length us, event | category | flops | bytes accessed | tf_op | source)
XLA Modules:
  0.0 176.6 jit_solution(17756275791275412283)
XLA Ops:
  0.6 163.0 %layer.1 = (bf16[2,256,768]{2,1,0:T(8,128)(2,1)}, bf16[2,256,768]{2,1,0:T(8,128)(2,1)}, bf16[96,3072]{1,0:T(8,128)(2,1)}, bf16[384,768]{1,0:T(8,128)(2,1)}, bf16...) custom-call(bf16[2,256,768]{2,1,0:T(8,128)(2,1)} %refs_0_.1, ...), custom_call_target="tpu_custom_call" | custom-call | tf_op jit(solution)/shard_map/layer/pallas_call | solution.py:955
  163.7 0.0 copy-start.2
  163.7 0.0 copy-start.1
  163.7 0.0 copy-start
  163.7 1.8 %convert_element_type.13 = f32[96,768]{1,0:T(8,128)} convert(bf16[96,768]{1,0:T(8,128)(2,1)} %get-tuple-element.33) | non-fusion elementwise | flops 73728 | bytes 442368 | tf_op jit(solution)/shard_map/convert_element_type | solution.py:970
  165.5 2.0 %convert_element_type.12 = f32[96,2304]{1,0:T(8,128)} convert(bf16[96,2304]{1,0:T(8,128)(2,1)} %get-tuple-element.32) | non-fusion elementwise | flops 221184 | bytes 1327104 | tf_op jit(solution)/shard_map/convert_element_type | solution.py:970
  167.5 0.0 copy-start.8
  167.5 0.0 copy-start.5
  167.5 0.0 copy-start.7
  167.5 2.2 %convert_element_type.14 = f32[96,3072]{1,0:T(8,128)} convert(bf16[96,3072]{1,0:T(8,128)(2,1)} %get-tuple-element.35) | non-fusion elementwise | flops 294912 | bytes 1769472 | tf_op jit(solution)/shard_map/convert_element_type | solution.py:970
  169.7 1.1 convert_element_type.15
  170.8 0.9 copy.37
  171.7 0.9 copy.38
  172.6 0.6 copy.39
  173.1 0.0 copy-done.3
  173.1 0.7 copy.40
  173.9 0.0 copy-done.4
  173.9 0.6 copy.41
  174.5 0.5 copy.42
  175.0 0.0 copy-done.8
  175.0 0.5 copy.43
  175.5 0.6 copy.44
  176.1 0.0 copy-done.7
  176.1 0.5 copy.45
  (10 shorter events, 0.0 us)
Async XLA Ops:
  163.7 6.1 %copy-start.2 = (bf16[384,768]{1,0:T(8,128)(2,1)S(1)}, bf16[384,768]{1,0:T(8,128)(2,1)}, u32[]{:S(2)}) copy-start(bf16[384,768]{1,0:T(8,128)(2,1)} %get-tuple-element.37) | copy-start | bytes 1769476
  163.7 7.1 %copy-start.1 = (bf16[2,256,768]{2,1,0:T(8,128)(2,1)S(1)}, bf16[2,256,768]{2,1,0:T(8,128)(2,1)}, u32[]{:S(2)}) copy-start(bf16[2,256,768]{2,1,0:T(8,128)(2,1)} %get-tuple-element.52) | copy-start | bytes 2359300
  163.7 8.0 %copy-start = (bf16[2,256,768]{2,1,0:T(8,128)(2,1)S(1)}, bf16[2,256,768]{2,1,0:T(8,128)(2,1)}, u32[]{:S(2)}) copy-start(bf16[2,256,768]{2,1,0:T(8,128)(2,1)} %get-tuple-element.53) | copy-start | bytes 2359300
  167.5 5.1 %copy-start.6 = (f32[2,128]{1,0:T(2,128)S(1)}, f32[2,128]{1,0:T(2,128)}, u32[]{:S(2)}) copy-start(f32[2,128]{1,0:T(2,128)} %get-tuple-element.54) | copy-start | bytes 3076
  167.5 5.7 %copy-start.3 = (f32[16,4608]{1,0:T(8,128)S(1)}, f32[16,4608]{1,0:T(8,128)}, u32[]{:S(2)}) copy-start(f32[16,4608]{1,0:T(8,128)} %get-tuple-element.55) | copy-start | bytes 884740
  167.5 6.4 %copy-start.4 = (f32[576]{0:T(1024)S(1)}, f32[576]{0:T(1024)}, u32[]{:S(2)}) copy-start(f32[576]{0:T(1024)} %get-tuple-element.56) | copy-start | bytes 6916
  167.5 7.0 %copy-start.9 = (f32[96]{0:T(128)S(1)}, f32[96]{0:T(128)}, u32[]{:S(2)}) copy-start(f32[96]{0:T(128)} %get-tuple-element.57) | copy-start | bytes 1156
  167.5 7.5 %copy-start.8 = (f32[96]{0:T(128)S(1)}, f32[96]{0:T(128)}, u32[]{:S(2)}) copy-start(f32[96]{0:T(128)} %get-tuple-element.60) | copy-start | bytes 1156
  167.5 8.0 %copy-start.5 = (f32[384]{0:T(512)S(1)}, f32[384]{0:T(512)}, u32[]{:S(2)}) copy-start(f32[384]{0:T(512)} %get-tuple-element.62) | copy-start | bytes 4612
  167.5 8.6 %copy-start.7 = (f32[96]{0:T(128)S(1)}, f32[96]{0:T(128)}, u32[]{:S(2)}) copy-start(f32[96]{0:T(128)} %get-tuple-element.64) | copy-start | bytes 1156

commit v3 on v2

--- a/solution.py
+++ b/solution.py
@@ -75,13 +75,13 @@
         con=V((uf, width), BF16), mod=V((8, width), F32),
         hid_a=V(whole, BF16), qq=V((pairs, total, PAIR), BF16), kk=V((pairs, total, PAIR), BF16),
         vv=V((pairs, total, PAIR), BF16), q_t=V((half, total), BF16),
-        est=V((2, span, total), BF16), inv_l=V((total, PAIR), F32),
+        lse=V((pairs, total, PAIR), F32),
         att_s=V((pairs, total, PAIR), BF16), att=V(piece, BF16),
         branch=V(piece, BF16), middle=V(piece, F32), hid_f=V(whole, BF16), gnar=V(whole, BF16),
         gbr=V(whole, BF16), act=V((total, ub), BF16), gwid=V((total, ub), BF16),
         nacc=V(whole, F32), hacc=V(whole, F32), nsend=V(piece, BF16),
         hsend=V(piece, BF16), hrecv=V(piece, BF16),
-        dom=V((total, PAIR), BF16), dom_t=V((PAIR, total), BF16), dsum=V((total, PAIR), F32),
+        dom_t=V((PAIR, total), BF16), dsum=V((total, PAIR), F32),
         dv_t=V((PAIR, total), F32), dk_t=V((PAIR, total), F32), dq=V((total, PAIR), F32),
         ge=V((2,) + two(4) + wide_strip, BF16), gc=V(two(4) + tall, BF16), gcs=V(two(2) + tall, BF16),
         gp=V(two(4) + half_strip, BF16), gps=V(two(3) + half_strip, BF16),
@@ -96,16 +96,54 @@
         ag_m=V(two(2) + (pairs + 1,) + half_strip, BF16),
         va=V((2, 16, half), F32), vb=V((2, 8, half), F32), va_r=V((16, half), F32), vb_r=V((8, half), F32),
         all_a=V((2, 16, 16, half), F32), all_b=V((2, 16, 8, half), F32), st=V((extent, 16), F32),
-        lsem=pltpu.SemaphoreType.DMA((64,)), esem=pltpu.SemaphoreType.DMA((2,)),
+        back=V((extent, 8), F32), total=V((1, 6 * width), F32),
+        cosine=V((total, PAIR), F32), sine=V((total, PAIR), F32), cond=V((2, extent), F32),
+        shifts=V((6 * width,), F32), prenorm=V((width,), F32), postnorm=V((width,), F32),
+        offsets=V((ff,), F32), baseline=V((width,), F32),
+        lsem=pltpu.SemaphoreType.DMA((64,)),
         ssem=pltpu.SemaphoreType.DMA((100,)), rsem=pltpu.SemaphoreType.DMA((100,)),
     )
 
 
+ORDERS = {
+    "E0": ("y", "x", "z", "q"),
+    "E1": ("z", "x", "y", "q"),
+    "P": ("z", "y", "x", "q"),
+    "M0": ("x", "z", "y", "q"),
+    "M1": ("z", "x", "y", "q"),
+    "M2": ("x", "z", "y", "q"),
+    "C": (("x", "y"), ("y", "x")),
+    "out": "b13",
+}
+SCHEDULE = (
+    ("f2", ("C0s",)),
+    ("n1", ("C1s",)),
+    ("gp", ("E0.0",)),
+    ("b00", ("Ps",)),
+    ("b01", ("gaC",)),
+    ("b02", ("C0.0", "E1.0")),
+    ("b10", ("E0.1", "P.0")),
+    ("b11", ("ga0", "C1.0")),
+    ("b13", ("E0.2",)),
+    ("b20", ("C0.1", "P.1", "M0.0")),
+    ("b21", ("ga1", "E1.1", "E0.3", "M1.0")),
+    ("b22", ("P.2",)),
+    ("b23", ("M0.1", "C1.1")),
+    ("l0", ("E1.2",)),
+    ("l1", ("P.3", "M0.2", "M1.1")),
+    ("tail", (
+        "ga2", "gbC", "M2.0", "C.2", "M0.3", "E1.3", "M1.2", "gb0",
+        "gb1", "M2.1", "ga3", "M1.3", "gaF", "gb2", "C.3", "agE",
+        "M2.2", "gb3", "agEc", "agP", "M2.3", "gbF", "agPc", "agC",
+        "agM", "agMc", "agCc",
+    )),
+)
+
 INPUTS = (
     "tok_h", "cot_h", "adap_h", "mix_h", "proj_h", "exp_h", "con_h",
-    "cond", "shifts", "prenorm", "postnorm", "offsets", "baseline", "cosine", "sine",
+    "cond_h", "shifts_h", "prenorm_h", "postnorm_h", "offsets_h", "baseline_h", "cosine_h", "sine_h",
 )
-GRADS = ("out_h", "gtok_h", "oe_h", "oc_h", "op_h", "om_h", "e_h")
+GRADS = ("out_h", "gtok_h", "oe_h", "oc_h", "op_h", "om_h")
 FINALS = ("time_o", "adaptive_o", "shifts_o", "prenorm_o", "postnorm_o", "offsets_o", "baseline_o")
 PARTIALS = ("all_a_h", "all_b_h")
 
@@ -173,9 +211,17 @@
     own_place = [rows_of(2 * j + c) for j in range(2)]
     other_place = [rows_of(2 * j + 1 - c) for j in range(2)]
 
+    barrier = pltpu.get_barrier_semaphore()
+    for dev in (core_dev, y_dev, dev0, dev1, dev2):
+        pl.semaphore_signal(barrier, inc=1, device_id=dev, device_id_type=MESH)
+
     adap_load = local(R.adap_h, R.adap)
     tok_load = local(R.tok_h.at[y], R.tok.at[y])
     cot_load = local(R.cot_h.at[y], R.cot.at[y])
+    first_loads = [
+        local(getattr(R, name + "_h"), getattr(R, name))
+        for name in ("cond", "shifts", "prenorm", "cosine", "sine", "postnorm", "offsets", "baseline")
+    ]
     mix_loads = []
     for j in range(pairs):
         for b in range(3):
@@ -186,13 +232,8 @@
     proj_load = local(R.proj_h, R.proj)
     exp_load = local(R.exp_h.at[:, pl.ds(pl.multiple_of(c * 2 * ub, PAIR), 2 * ub)], R.exp)
     con_load = local(R.con_h.at[pl.ds(pl.multiple_of(c * 2 * ub, PAIR), 2 * ub), :], R.con)
-    for item in [adap_load, tok_load, cot_load] + mix_loads + [proj_load, exp_load, con_load]:
+    for item in [adap_load, tok_load] + first_loads + mix_loads:
         item.start()
-
-    barrier = pltpu.get_barrier_semaphore()
-    for dev in (core_dev, y_dev, dev0, dev1, dev2):
-        pl.semaphore_signal(barrier, inc=1, device_id=dev, device_id_type=MESH)
-    pl.semaphore_wait(barrier, 5)
 
     tok_swap = link(R.tok_h.at[1 - y], R.tok.at[y], y_dev)
     cot_swap = link(R.cot_h.at[1 - y], R.cot.at[y], y_dev)
@@ -236,8 +277,7 @@
             self.steps[t][0].start()
 
         def land(self, t, into=None):
-            item, place, recv = self.steps[t]
-            item.wait_recv()
+            _, place, recv = self.steps[t]
             value = self.acc.at[place][...] + recv[...]
             if into is None:
                 self.acc.at[place][...] = value
@@ -259,88 +299,152 @@
             rows = (16 >> len(bits)) * strip
             return self.ref.at[pl.ds(pl.multiple_of(start * strip, strip), rows), self.lanes]
 
-    x_step, z_step, y_step, q_step = (b0, dev0), (b1, dev1), (y, y_dev), (b2, dev2)
-    sum_e = [
-        Halving(R.ge.at[i], [z_step + (R.e1.at[i],), y_step + (R.e2.at[i],), x_step + (R.e3.at[i],), q_step + (R.e4.at[i],)])
-        for i in range(2)
-    ]
-    sum_m = [
-        Halving(Strips(R.exp, pl.ds(j * half, half)), [x_step + (R.m1.at[j],), z_step + (R.m2.at[j],), y_step + (R.m3.at[j],), q_step + (R.m4.at[j],)])
-        for j in range(pairs)
-    ]
-    swap_p = link(R.gps, R.gp.at[:, :, :, c], core_dev)
-    sum_p = Halving(R.gp, [y_step + (R.p1,), x_step + (R.p2,), z_step + (R.p3,), q_step + (R.p4,)])
-    swap_c = [link(R.gcs, R.gc.at[:, :, i, c], core_dev) for i in range(2)]
-    first_c = [link(R.gc.at[1 - b0, :, i], R.c1.at[i], dev0) for i in range(2)]
-    second_c = [link(R.gc.at[b0, 1 - y, i], R.c2.at[i], y_dev) for i in range(2)]
-    third_c = link(R.gc.at[b0, y, 1 - b1], R.c3, dev1)
-    fourth_c = link(R.gc.at[b0, y, b1, 1 - b2], R.c4, dev2)
-
-    def land_c1(i):
-        first_c[i].wait_recv()
-        R.gc[b0, :, i] = R.gc[b0, :, i] + R.c1[i]
-
-    def land_c2(i):
-        second_c[i].wait_recv()
-        R.gc[b0, y, i] = R.gc[b0, y, i] + R.c2[i]
+    step_of = dict(x=(b0, dev0), y=(y, y_dev), z=(b1, dev1), q=(b2, dev2))
+
+    def steps_of(order, recvs):
+        return [step_of[key] + (recv,) for key, recv in zip(order, recvs)]
+
+    sums = {
+        "E0": Halving(R.ge.at[0], steps_of(ORDERS["E0"], [r.at[0] for r in (R.e1, R.e2, R.e3, R.e4)])),
+        "E1": Halving(R.ge.at[1], steps_of(ORDERS["E1"], [r.at[1] for r in (R.e1, R.e2, R.e3, R.e4)])),
+        "P": Halving(R.gp, steps_of(ORDERS["P"], (R.p1, R.p2, R.p3, R.p4))),
+    }
+    for j in range(pairs):
+        sums[f"M{j}"] = Halving(
+            Strips(R.exp, pl.ds(j * half, half)),
+            steps_of(ORDERS[f"M{j}"], [r.at[j] for r in (R.m1, R.m2, R.m3, R.m4)]),
+        )
+    links, lands = {}, {}
+    finals = {
+        "E0": R.ag_e.at[c, y, 0], "E1": R.ag_e.at[c, y, 1], "P": R.ag_m.at[c, y, 0],
+        **{f"M{j}": R.ag_m.at[c, y, 1 + j] for j in range(pairs)},
+    }
+    for name, item in sums.items():
+        for t in range(4):
+            links[f"{name}.{t}"] = item.steps[t][0]
+            lands[f"{name}.{t}"] = functools.partial(item.land, t, finals[name] if t == 3 else None)
+
+    everything = slice(None)
+
+    def place_c(i, **bits):
+        return (bits.get("x", everything), bits.get("y", everything), i)
+
+    def land_c(link_name, place, recv):
+        def run():
+            R.gc[place] = R.gc[place] + recv[...]
+
+        lands[link_name] = run
+
+    def link_c(name, send_place, keep_place, recv, dev):
+        links[name] = link(R.gc.at[send_place], recv, dev)
+        land_c(name, keep_place, recv)
+
+    own_bit = dict(x=b0, y=y)
+    plan_c = ORDERS["C"]
+    for i in range(2):
+        links[f"C{i}s"] = link(R.gcs, R.gc.at[:, :, i, c], core_dev)
+        lands[f"C{i}s"] = lambda: None
+        one, two = plan_c[i]
+        link_c(
+            f"C{i}.0", place_c(i, **{one: 1 - own_bit[one]}), place_c(i, **{one: own_bit[one]}),
+            R.c1.at[i], step_of[one][1],
+        )
+        if len(plan_c) == 2:
+            link_c(
+                f"C{i}.1", place_c(i, **{one: own_bit[one], two: 1 - own_bit[two]}), place_c(i, **own_bit),
+                R.c2.at[i], step_of[two][1],
+            )
+    if len(plan_c) == 2:
+        link_c("C.2", place_c(1 - b1, **own_bit), place_c(b1, **own_bit), R.c3, dev1)
+    else:
+        link_c(
+            "C.1", place_c(1 - b1, **{one: own_bit[one]}), place_c(b1, **{one: own_bit[one]}), R.c2, dev1
+        )
+        link_c(
+            "C.2", place_c(b1, **{one: own_bit[one], two: 1 - own_bit[two]}), place_c(b1, **own_bit),
+            R.c3, step_of[two][1],
+        )
+    links["C.3"] = link(R.gc.at[b0, y, b1, 1 - b2], R.c4, dev2)
 
     def land_c3():
-        third_c.wait_recv()
-        R.gc[b0, y, b1] = R.gc[b0, y, b1] + R.c3[...]
-
-    def land_c4():
-        fourth_c.wait_recv()
         R.ag_c[c, y] = R.gc[b0, y, b1, b2] + R.c4[...]
 
-    y_e, core_e = link(R.ag_e.at[c, y], R.ag_e.at[c, y], y_dev), link(R.ag_e.at[c], R.ag_e.at[c], core_dev)
-    y_c, core_c = link(R.ag_c.at[c, y], R.ag_c.at[c, y], y_dev), link(R.ag_c.at[c], R.ag_c.at[c], core_dev)
+    lands["C.3"] = land_c3
+    links["Ps"] = link(R.gps, R.gp.at[:, :, :, c], core_dev)
     most, last = pl.ds(0, pairs), pl.ds(pairs, 1)
-    y_m, core_m = [], []
-    for part in (most, last):
-        y_m.append(link(R.ag_m.at[c, y, part], R.ag_m.at[c, y, part], y_dev))
-        core_m.append(link(R.ag_m.at[c, :, part], R.ag_m.at[c, :, part], core_dev))
+    for name, mine, both in (
+        ("agE", R.ag_e.at[c, y], R.ag_e.at[c]),
+        ("agC", R.ag_c.at[c, y], R.ag_c.at[c]),
+        ("agP", R.ag_m.at[c, y, most], R.ag_m.at[c, :, most]),
+        ("agM", R.ag_m.at[c, y, last], R.ag_m.at[c, :, last]),
+    ):
+        links[name] = link(mine, mine, y_dev)
+        links[name + "c"] = link(both, both, core_dev)
+
+    chip = b0 * 8 + b2 * 4 + b1 * 2 + y
+
+    def land_total(part, recv, every):
+        def run():
+            every[c, chip] = part[c] + recv[...]
+
+        return run
+
+    for name, part, recv, every in (("ga", R.va, R.va_r, R.all_a), ("gb", R.vb, R.vb_r, R.all_b)):
+        links[name + "C"] = link(part.at[1 - c], recv, core_dev)
+        lands[name + "C"] = land_total(part, recv, every)
+        for t, dev in enumerate((y_dev, dev1, dev2, dev0)):
+            size = 2**t
+            ref = every.at[c, pl.ds(lax.div(chip, size) * size, size)]
+            links[f"{name}{t}"] = link(ref, ref, dev)
+        links[name + "F"] = link(every.at[c], every.at[c], core_dev)
+
+    sequence = [name for _, landed in SCHEDULE for name in landed]
+    follow = {"C0s": "C0.0", "C1s": "C1.0", "Ps": "P.0", "C.2": "C.3", "C.3": "agC"}
+    for name in ("agE", "agC", "agP", "agM"):
+        follow[name] = name + "c"
+    for name in ("ga", "gb"):
+        for one, two in zip("C0123", "0123F"):
+            follow[name + one] = name + two
+    for name in sums:
+        for t in range(3):
+            follow[f"{name}.{t}"] = f"{name}.{t + 1}"
+    if len(plan_c) == 2:
+        follow.update({"C0.0": "C0.1", "C1.0": "C1.1"})
+        joined = [(("C0.1", "C1.1"), "C.2")]
+    else:
+        follow["C.1"] = "C.2"
+        joined = [(("C0.0", "C1.0"), "C.1")]
+    joined += [(("E0.3", "E1.3"), "agE"), (("P.3", "M0.3", "M1.3"), "agP"), (("M2.3",), "agM")]
+    for names_in, name in joined:
+        follow[max(names_in, key=sequence.index)] = name
+
+    def serve(name):
+        links[name].wait_recv()
+        if name in lands:
+            lands[name]()
+        if name in follow:
+            links[follow[name]].start()
+
+    def service(point):
+        for name in dict(SCHEDULE).get(point, ()):
+            if name == "out":
+                continue
+            serve(name)
 
     def add_row(ref, r, value):
         for n in range(2):
             ref[n, pl.ds(r, 1), :] += value[:, n * half : (n + 1) * half]
 
-    chip = y * 8 + hi
-
-    class Gather:
-        def __init__(self, part, recv, every):
-            self.part, self.recv, self.every = part, recv, every
-            self.first = link(part.at[1 - c], recv, core_dev)
-            self.steps = []
-            for t, dev in enumerate((dev0, dev1, dev2, y_dev)):
-                size = 2**t
-                start = lax.div(chip, size) * size
-                ref = every.at[c, pl.ds(start, size)]
-                self.steps.append(link(ref, ref, dev))
-            self.steps.append(link(every.at[c], every.at[c], core_dev))
-
-        def start(self):
-            self.first.start()
-
-        def step(self, t):
-            if t == 0:
-                self.first.wait_recv()
-                self.every[c, chip] = self.part[c] + self.recv[...]
-            else:
-                self.steps[t - 1].wait_recv()
-            self.steps[t].start()
-
-        def finish(self):
-            self.steps[-1].wait_recv()
-
-    gather_a = Gather(R.va, R.va_r, R.all_a)
-    gather_b = Gather(R.vb, R.vb_r, R.all_b)
-
+    pl.semaphore_wait(barrier, 5)
     tok_swap.start()
-    cot_swap.start()
+    for item in (cot_load, proj_load, exp_load, con_load):
+        item.start()
     R.va[...] = jnp.zeros_like(R.va)
     R.vb[...] = jnp.zeros_like(R.vb)
 
     adap_load.wait()
+    for item in first_loads:
+        item.wait()
     crow = jnp.where(y == 0, R.cond[0:1, :], R.cond[1:2, :])
     crow = crow * (1.0 / (1.0 + jnp.exp(-crow)))
     extent = crow.shape[1]
@@ -393,17 +497,7 @@
     for j in range(pairs):
         R.q_t[j * PAIR : (j + 1) * PAIR, :] = R.qq[j].T
 
-    cot_load.wait()
-    cot_swap.wait_recv()
-    for j in range(2):
-        low = (R.cot[j].astype(F32) * R.mod[5:6, :]).astype(BF16)
-        R.gnar[own_place[j], :] = low
-        add_row(R.va, 5, column_sum(low.astype(F32)))
-        gnar_push[j].start()
-
-    def e_copy(n, slot):
-        return pltpu.make_async_copy(R.est.at[slot], R.e_h.at[n], R.esem.at[slot])
-
+    cot_swap.start()
     def att_push(j, jj):
         lanes = pl.ds(pl.multiple_of(c * half + j * PAIR, PAIR), PAIR)
         return remote(
@@ -430,30 +524,19 @@
         score = score_of(*steps[0])
         for index, (hh, qb) in enumerate(steps):
             following = score_of(*steps[index + 1]) if index + 1 < len(steps) else None
-            n = j * (2 * blocks) + index
-            slot = index % 2
             place = slice(qb * span, (qb + 1) * span)
             top = jnp.max(score, axis=1, keepdims=True)
             low = jnp.exp(score - top).astype(BF16)
-            if index < 2:
-                @pl.when(j > 0)
-                def _():
-                    e_copy(n, slot).wait()
-            else:
-                e_copy(n, slot).wait()
-            R.est[slot] = low
-            e_copy(n, slot).start()
             grown = dot(low, values[hh])
-            inverse = 1.0 / pltpu.roll(grown, HDIM, 1)
-            grown = (grown * inverse).astype(BF16)
-            head_lane = 0 if hh == 0 else HDIM
-            R.inv_l[place, :] = jnp.where(
-                lane_pair == 2 * j + hh, inverse[:, head_lane : head_lane + 1], R.inv_l[place, :]
-            )
+            totals = pltpu.roll(grown, HDIM, 1)
+            grown = (grown / totals).astype(BF16)
+            weight = top + jnp.log(totals)
             if hh == 0:
                 R.att_s[j, place, :] = grown
+                R.lse[j, place, :] = weight
             else:
                 R.att_s[j, place, :] = jnp.where(lane_pair < HDIM, R.att_s[j, place, :], grown)
+                R.lse[j, place, :] = jnp.where(lane_pair < HDIM, R.lse[j, place, :], weight)
             score = following
         lanes = pl.ds(pl.multiple_of(c * half + j * PAIR, PAIR), PAIR)
         for jj in range(2):
@@ -461,10 +544,15 @@
             R.att[jj, :, lanes] = R.att_s[j, own_place[jj], :]
         return carry
 
-    R.inv_l[...] = jnp.zeros_like(R.inv_l)
     lax.fori_loop(0, pairs, attend, 0)
-    for slot in range(2):
-        e_copy(0, slot).wait()
+    cot_load.wait()
+    cot_swap.wait_recv()
+    for j in range(2):
+        low = (R.cot[j].astype(F32) * R.mod[5:6, :]).astype(BF16)
+        R.gnar[own_place[j], :] = low
+        add_row(R.va, 5, column_sum(low.astype(F32)))
+        gnar_push[j].start()
+
     for j in range(pairs):
         for jj in range(2):
             att_push(j, jj).wait_recv()
@@ -478,6 +566,10 @@
         normal, _ = normalize(value)
         R.hid_f[own_place[j], :] = (normal * (postgain * (1.0 + R.mod[4:5, :])) + R.mod[3:4, :]).astype(BF16)
         hid_f_push[j].start()
+
+    def bits_of(n, order):
+        bits = dict(q=n // 8, z=n // 4 % 2, x=n // 2 % 2, y=n % 2)
+        return tuple(bits[key] for key in order)
 
     exp_load.wait()
     con_load.wait()
@@ -496,10 +588,11 @@
                     remote(R.hid_f.at[place, :], R.hid_f.at[place, :], hid_f_base + j, core_dev).wait_recv()
                     remote(R.gnar.at[place, :], R.gnar.at[place, :], gnar_base + j, core_dev).wait_recv()
             else:
-                @pl.when(t == 1)
-                def _():
-                    swap_c[0].wait_recv()
-                    first_c[0].start()
+                for k in range(1, 4):
+                    if f"f{k - 1}" in dict(SCHEDULE):
+                        @pl.when(t == k)
+                        def _(k=k):
+                            service(f"f{k - 1}")
             v = dot(R.hid_f[place, :], R.exp[:, units]) + offsets[:, i * ub : (i + 1) * ub]
             square = v * v
             th = jnp.tanh(v * (GELU_A + (GELU_A * GELU_B) * square))
@@ -533,20 +626,22 @@
                 item.open = True
         value = dot(R.hid_f[...], R.gwid[...], COLS_BY_COLS).astype(BF16)
         for n in range(16):
-            a2, a1, a0, ay = n // 8, n // 4 % 2, n // 2 % 2, n % 2
-            R.ge[i, a1, ay, a0, a2] = value[n * strip : (n + 1) * strip]
-        sum_e[i].send(0)
+            R.ge[(i,) + bits_of(n, ORDERS[f"E{i}"])] = value[n * strip : (n + 1) * strip]
+        links[f"E{i}.0"].start()
+        service(f"E{i}")
         value = dot(R.act[...], R.gnar[...], COLS_BY_COLS).astype(BF16)
         left, right = value[:, :half], value[:, half:]
         mine = jnp.where(c == 0, left, right)
         theirs = jnp.where(c == 0, right, left)
         if i == 1:
-            swap_c[0].wait_send()
+            service("f3")
+            links["C0s"].wait_send()
         for n in range(4):
             a0, ay = n // 2, n % 2
             R.gcs[a0, ay] = theirs[n * block : (n + 1) * block]
             R.gc[a0, ay, i, c] = mine[n * block : (n + 1) * block]
-        swap_c[i].start()
+        links[f"C{i}s"].start()
+        service(f"C{i}")
 
     base_row = R.baseline[...].reshape(1, width)
     for j in range(2):
@@ -569,20 +664,18 @@
         R.gbr[place, :] = (R.mod[2:3, :] * value).astype(BF16)
         gbr_push[j].start()
         if j == 0:
-            swap_c[1].wait_recv()
-            first_c[1].start()
+            service("n0")
 
     out_local = local(stage(0, y), R.out_h.at[y])
     out_local.start()
-    out_push.start()
-    gather_a.start()
+    links["gaC"].start()
+    out_at = ORDERS["out"]
+    if out_at == "n1":
+        out_push.start()
+    service("n1")
     for j in range(2):
         gbr_push[j].wait_recv()
 
-    def e_back(n, slot):
-        return pltpu.make_async_copy(R.e_h.at[n], R.est.at[slot], R.esem.at[slot])
-
-    e_back(0, 0).start()
     value = jnp.concatenate(
         [dot(R.att_s[j], R.gbr[...], COLS_BY_COLS).astype(BF16) for j in range(pairs)], axis=0
     )
@@ -590,122 +683,60 @@
     mine = jnp.where(c == 0, left, right)
     theirs = jnp.where(c == 0, right, left)
     for n in range(8):
-        a1, a0, ay = n // 4, n // 2 % 2, n % 2
-        R.gps[ay, a0, a1] = theirs[n * strip : (n + 1) * strip]
-        R.gp[ay, a0, a1, c] = mine[n * strip : (n + 1) * strip]
-    swap_p.start()
-    sum_e[0].land(0)
-    sum_e[0].send(1)
-
-    def m_first(j):
-        return lambda: sum_m[j].send(0)
-
-    def forward(item, t, into=None):
-        def run():
-            item.land(t, into)
-            if into is None:
-                item.send(t + 1)
-        return run
-
-    def c_second(i):
-        def run():
-            land_c1(i)
-            second_c[i].start()
-        return run
-
-    def c_third():
-        land_c2(0)
-        land_c2(1)
-        third_c.start()
-
-    def c_fourth():
-        land_c3()
-        fourth_c.start()
-
-    def c_last():
-        land_c4()
-        y_c.start()
-
-    def c_core():
-        y_c.wait_recv()
-        core_c.start()
-
-    def e_y():
-        y_e.start()
-
-    def e_core():
-        y_e.wait_recv()
-        core_e.start()
-
-    def p_first():
-        swap_p.wait_recv()
-        sum_p.send(0)
-
-    final_e = [R.ag_e.at[c, y, i] for i in range(2)]
-    final_m = [R.ag_m.at[c, y, 1 + j] for j in range(pairs)]
-    final_p = R.ag_m.at[c, y, 0]
-    schedule = {
-        (0, 0): [p_first, lambda: gather_a.step(0)],
-        (0, 1): [c_second(0), lambda: gather_a.step(1)],
-        (0, 2): [m_first(0), forward(sum_e[0], 1)],
-        (1, 0): [forward(sum_e[1], 0), lambda: gather_a.step(2)],
-        (1, 1): [c_second(1), forward(sum_p, 0), lambda: gather_a.step(3)],
-        (1, 2): [m_first(1), forward(sum_e[0], 2)],
-        (2, 0): [forward(sum_e[1], 1), forward(sum_m[0], 0), forward(sum_p, 1), lambda: gather_a.step(4)],
-        (2, 1): [c_third, forward(sum_e[0], 3, final_e[0]), forward(sum_p, 2)],
-        (2, 2): [m_first(2), forward(sum_e[1], 2), forward(sum_m[0], 1), forward(sum_m[1], 0)],
-    }
-
-    def service(j, point):
-        for k in range(pairs):
-            tasks = schedule.get((k, point), [])
-            if tasks:
-                @pl.when(j == k)
-                def _(tasks=tasks):
-                    for task in tasks:
-                        task()
-
+        place = bits_of(n, ORDERS["P"][:3])
+        R.gps[place] = theirs[n * strip : (n + 1) * strip]
+        R.gp[place + (c,)] = mine[n * strip : (n + 1) * strip]
+    links["Ps"].start()
     own_proj = R.proj[pl.ds(pl.multiple_of(c * half, PAIR), half), :]
     grown = dot(R.gbr[...], own_proj, ROWS_BY_ROWS).astype(BF16)
     for j in range(pairs):
         R.act[:, half + j * PAIR : half + (j + 1) * PAIR] = grown[:, j * PAIR : (j + 1) * PAIR]
 
+    if out_at == "gp":
+        out_push.start()
+    service("gp")
+
+
+    def service_pair(j, point):
+        for k in range(pairs):
+            key = f"b{k}{point}"
+            if key == out_at or key in dict(SCHEDULE):
+                @pl.when(j == k)
+                def _(key=key):
+                    if key == out_at:
+                        out_push.start()
+                    service(key)
+
     def attend_back(j, carry):
         grown = R.act[:, pl.ds(pl.multiple_of(half + j * PAIR, PAIR), PAIR)].astype(F32)
         product = grown * R.att_s[j].astype(F32)
-        table = R.inv_l[...]
-        inverse, inner = [], []
-        for hh in range(2):
-            inverse.append(jnp.sum(jnp.where(lane_long == 2 * j + hh, table, 0.0), axis=1, keepdims=True))
-            inner.append(jnp.sum(jnp.where(in_head(lane_long, hh), product, 0.0), axis=1, keepdims=True))
-        inverse = jnp.where(in_head(lane_long, 0), inverse[0], inverse[1])
-        R.dsum[...] = jnp.where(in_head(lane_long, 0), inner[0], inner[1]) * inverse
-        grown = (grown * inverse).astype(BF16)
-        R.dom[...] = grown
-        R.dom_t[...] = grown.T
-
-        def grad_of(hh, qb):
-            there = R.dom[qb * span : (qb + 1) * span, :]
-            there = jnp.where(in_head(lane_pair, hh), there, jnp.zeros_like(there))
-            return dot(there, R.vv[j], ROWS_BY_ROWS)
+        inner = [
+            jnp.sum(jnp.where(in_head(lane_long, hh), product, 0.0), axis=1, keepdims=True) for hh in range(2)
+        ]
+        R.dsum[...] = jnp.where(in_head(lane_long, 0), inner[0], inner[1])
+        R.dom_t[...] = grown.astype(BF16).T
+
+        lanes = pl.ds(pl.multiple_of(half + j * PAIR, PAIR), PAIR)
+
+        def one_head(value, hh):
+            return jnp.where(in_head(lane_pair, hh), value, jnp.zeros_like(value))
+
+        def products(hh, qb):
+            rows = slice(qb * span, (qb + 1) * span)
+            grad = dot(one_head(R.act[rows, lanes], hh), R.vv[j], ROWS_BY_ROWS)
+            return grad, dot(one_head(R.qq[j, rows, :], hh), R.kk[j], ROWS_BY_ROWS)
 
         steps = [(hh, qb) for hh in range(2) for qb in range(blocks)]
-        grad = grad_of(*steps[0])
+        current = products(*steps[0])
         for index, (hh, qb) in enumerate(steps):
-            following = grad_of(*steps[index + 1]) if index + 1 < len(steps) else None
-            n = j * (2 * blocks) + index
-            slot = index % 2
-            e_back(n, slot).wait()
-            if index + 1 == len(steps):
-                @pl.when(j < pairs - 1)
-                def _():
-                    e_back(n + 1, 1 - slot).start()
-            else:
-                e_back(n + 1, 1 - slot).start()
+            following = products(*steps[index + 1]) if index + 1 < len(steps) else None
+            grad, score = current
             place = slice(qb * span, (qb + 1) * span)
             rows = slice(hh * HDIM, (hh + 1) * HDIM)
-            low = R.est[slot]
-            grad = (low.astype(F32) * (grad - R.dsum[place, hh * HDIM : hh * HDIM + 1])).astype(BF16)
+            first = hh * HDIM
+            weight = jnp.exp(score - R.lse[j, place, first : first + 1])
+            low = weight.astype(BF16)
+            grad = (weight * (grad - R.dsum[place, first : first + 1])).astype(BF16)
             q_part = dot(grad, R.kk[j])
             v_part = dot(R.dom_t[rows, place], low)
             k_part = dot(R.q_t[pl.ds(pl.multiple_of(j * PAIR + hh * HDIM, HDIM), HDIM), place], grad)
@@ -720,8 +751,8 @@
                 R.dv_t[rows, :] += v_part
                 R.dk_t[rows, :] += k_part
             if qb == blocks - 1:
-                service(j, hh)
-            grad = following
+                service_pair(j, hh)
+            current = following
         gq = R.dq[...] * HDIM ** (-0.5)
         gk = R.dk_t[...].T
         gmx = R.act.at[:, pl.ds(0, 3 * PAIR)]
@@ -729,13 +760,18 @@
         gmx[:, PAIR : 2 * PAIR] = (gk * R.cosine[...] - turn(gk) * R.sine[...]).astype(BF16)
         gmx[:, 2 * PAIR :] = R.dv_t[...].astype(BF16).T
         value = dot(R.hid_a[...], gmx[...], COLS_BY_COLS).astype(BF16)
-        for n in range(16):
-            a2, a1, a0, ay = n // 8, n // 4 % 2, n // 2 % 2, n % 2
-            index = ((a0 * 2 + a1) * 2 + ay) * 2 + a2
-            R.exp[index * strip : (index + 1) * strip, pl.ds(pl.multiple_of(j * half, PAIR), half)] = value[
-                n * strip : (n + 1) * strip
-            ]
-        service(j, 2)
+        for k in range(pairs):
+            @pl.when(j == k)
+            def _(k=k):
+                for n in range(16):
+                    index = 0
+                    for bit in bits_of(n, ORDERS[f"M{k}"]):
+                        index = 2 * index + bit
+                    R.exp[index * strip : (index + 1) * strip, k * half : (k + 1) * half] = value[
+                        n * strip : (n + 1) * strip
+                    ]
+                links[f"M{k}.0"].start()
+        service_pair(j, 2)
         lanes = pl.ds(pl.multiple_of(j * 3 * PAIR, PAIR), 3 * PAIR)
 
         def back(p, inner):
@@ -753,6 +789,7 @@
             return inner
 
         lax.fori_loop(0, blocks, back, 0)
+        service_pair(j, 3)
         return carry
 
     lax.fori_loop(0, pairs, attend_back, 0)
@@ -761,8 +798,6 @@
         R.hsend[j] = R.hacc[other_place[j], :].astype(BF16)
         asum_push[j].start()
 
-    forward(sum_p, 3, final_p)()
-    c_fourth()
     gtok_local = local(stage(1, y), R.gtok_h.at[y])
     for j, item in ((1 - y, gtok_push), (y, gtok_local)):
         got = R.hacc[rows_of(2 * j + c), :] + 0.0
@@ -779,32 +814,13 @@
             R.middle[j] + normalize_back(got * (pregain * (1.0 + R.mod[1:2, :])), normal, scale)
         ).astype(BF16)
         item.start()
-    gather_b.start()
-    forward(sum_e[1], 3, final_e[1])()
-    e_y()
-    forward(sum_m[0], 2)()
-    forward(sum_m[1], 1)()
-    forward(sum_m[2], 0)()
-    gather_b.step(0)
-    c_last()
-    forward(sum_m[0], 3, final_m[0])()
-    forward(sum_m[1], 2)()
-    forward(sum_m[2], 1)()
-    gather_b.step(1)
-    e_core()
-    forward(sum_m[1], 3, final_m[1])()
-    y_m[0].start()
-    forward(sum_m[2], 2)()
-    gather_b.step(2)
-    c_core()
-    forward(sum_m[2], 3, final_m[2])()
-    y_m[1].start()
-    gather_b.step(3)
-    y_m[0].wait_recv()
-    core_m[0].start()
-    gather_b.step(4)
-    y_m[1].wait_recv()
-    core_m[1].start()
+        if item is gtok_push:
+            if out_at == "l0":
+                out_push.start()
+            service("l0")
+    links["gbC"].start()
+    service("l1")
+    service("l2")
 
     stores = []
 
@@ -813,42 +829,65 @@
         item.start()
         stores.append(item)
 
-    core_e.wait_recv()
-    for n in range(8):
-        cc, yy, i = n // 4, n // 2 % 2, n % 2
-        store(
-            R.ag_e.at[cc, yy, i],
-            R.oe_h.at[pl.ds(yy * strip, strip), pl.ds((2 * cc + i) * width, width)],
-        )
-    core_c.wait_recv()
-    for n in range(4):
-        cc, yy = n // 2, n % 2
-        store(R.ag_c.at[cc, yy], R.oc_h.at[pl.ds(yy * block, block), pl.ds(cc * half, half)])
-    gather_a.finish()
-    gather_b.finish()
-    if leftover == 1:
-        finish_vectors(R, hi, width, half, extent)
-    else:
-        store(R.all_a, R.all_a_h)
-        store(R.all_b, R.all_b_h)
-    core_m[0].wait_recv()
-    for n in range(4):
-        cc, yy = n // 2, n % 2
-        store(R.ag_m.at[cc, yy, 0], R.op_h.at[pl.ds(yy * strip, strip), pl.ds(cc * half, half)])
-    core_m[1].wait_recv()
-    for item in hid_f_push:
-        item.open = True
-        item.wait_send()
-    for n in range(4):
-        cc, yy = n // 2, n % 2
-        for j in range(pairs):
+    def store_e():
+        for n in range(8):
+            cc, yy, i = n // 4, n // 2 % 2, n % 2
+            store(
+                R.ag_e.at[cc, yy, i],
+                R.oe_h.at[pl.ds(yy * strip, strip), pl.ds((2 * cc + i) * width, width)],
+            )
+
+    def store_c():
+        for n in range(4):
+            cc, yy = n // 2, n % 2
+            store(R.ag_c.at[cc, yy], R.oc_h.at[pl.ds(yy * block, block), pl.ds(cc * half, half)])
+
+    def place_m(j):
+        for n in range(4):
+            cc, yy = n // 2, n % 2
             value = R.ag_m[cc, yy, 1 + j]
             for b in range(3):
                 lane = cc * half + j * PAIR
                 row = (2 * b + yy) * strip
                 R.hid_f[row : row + strip, lane : lane + PAIR] = value[:, b * PAIR : (b + 1) * PAIR]
-    for b in range(3):
-        store(R.hid_f.at[pl.ds(2 * b * strip, 2 * strip), :], R.om_h.at[:, pl.ds(b * width, width)])
+
+    def store_p():
+        for n in range(4):
+            cc, yy = n // 2, n % 2
+            store(R.ag_m.at[cc, yy, 0], R.op_h.at[pl.ds(yy * strip, strip), pl.ds(cc * half, half)])
+        for item in hid_f_push:
+            item.open = True
+            item.wait_send()
+        for j in range(pairs - 1):
+            place_m(j)
+
+    def store_m():
+        place_m(pairs - 1)
+        for b in range(3):
+            store(R.hid_f.at[pl.ds(2 * b * strip, 2 * strip), :], R.om_h.at[:, pl.ds(b * width, width)])
+
+    results = {"agEc": store_e, "agCc": store_c, "agPc": store_p, "agMc": store_m}
+    if leftover == 1:
+        early, later = finish_vectors(R, hi, chip - y, width, half, extent)
+    else:
+        early = [lambda: store(R.all_a, R.all_a_h)]
+        later = [lambda: store(R.all_b, R.all_b_h)]
+    pieces = []
+    tail = dict(SCHEDULE)["tail"]
+    if "gaF" not in tail:
+        pieces.extend(early)
+    for name in tail:
+        serve(name)
+        if name in results:
+            results[name]()
+        if name == "gaF":
+            pieces.extend(early)
+        if name == "gbF":
+            pieces.extend(later)
+        if pieces:
+            pieces.pop(0)()
+    for piece in pieces:
+        piece()
     for item in stores:
         item.wait()
     out_local.wait()
@@ -863,32 +902,26 @@
             item.wait_send()
 
 
-def finish_vectors(R, hi, width, half, extent):
+def finish_vectors(R, hi, chip, width, half, extent):
     own = extent // 8
     highest = lax.Precision.HIGHEST
-    R.st[...] = R.all_a[0, :, 10, :extent].T
-    silu_own = R.st[pl.ds(pl.multiple_of(hi * own, own), own), :]
     sections = ((R.all_b, 0), (R.all_b, 1), (R.all_a, 0), (R.all_a, 1), (R.all_a, 2), (R.all_a, 3))
-    sums = []
-    back = [jnp.zeros((extent, 1), F32) for _ in range(2)]
-    for n, (ref, r) in enumerate(sections):
-        for h in range(2):
-            grads = ref[h, :, r, :]
-            lanes = pl.ds(n * width + h * half, half)
-            R.adaptive_o[:, lanes] = jnp.dot(silu_own, grads, precision=highest, preferred_element_type=F32)
-            sums.append(column_sum(grads))
-            table = R.adap[:, lanes].astype(F32)
-            for yy in range(2):
-                mine = ref[h, pl.ds(yy * 8 + hi, 1), r, :]
-                back[yy] = back[yy] + jnp.sum(table * mine, axis=1, keepdims=True)
-    eye = lax.broadcasted_iota(jnp.int32, (extent, extent), 0) == lax.broadcasted_iota(
-        jnp.int32, (extent, extent), 1
-    )
-    for yy in range(2):
-        row = column_sum(jnp.where(eye, jnp.broadcast_to(back[yy], (extent, extent)), 0.0))
-        cond = R.cond[yy : yy + 1, :]
-        gate = 1.0 / (1.0 + jnp.exp(-cond))
-        R.time_o[yy : yy + 1, :] = row * (gate * (1.0 + cond * (1.0 - gate)))
+
+    def transpose():
+        R.st[...] = R.all_a[0, :, 10, :extent].T
+        R.back[...] = jnp.zeros_like(R.back)
+
+    def section(n, h):
+        ref, r = sections[n]
+        grads = ref[h, :, r, :]
+        lanes = pl.ds(n * width + h * half, half)
+        silu_own = R.st[pl.ds(pl.multiple_of(hi * own, own), own), :]
+        R.adaptive_o[:, lanes] = jnp.dot(silu_own, grads, precision=highest, preferred_element_type=F32)
+        R.total[:, lanes] = column_sum(grads)
+        table = R.adap[:, lanes].astype(F32)
+        for yy in range(2):
+            mine = ref[h, pl.ds(chip + yy, 1), r, :]
+            R.back[:, yy : yy + 1] += jnp.sum(table * mine, axis=1, keepdims=True)
 
     def share(vector, out):
         size = vector.shape[1] // 8
@@ -900,11 +933,59 @@
     def total_of(ref, r):
         return jnp.concatenate([column_sum(ref[h, :, r, :]) for h in range(2)], axis=1)
 
-    share(jnp.concatenate(sums, axis=1), R.shifts_o)
-    share(total_of(R.all_b, 2), R.prenorm_o)
-    share(total_of(R.all_a, 4), R.postnorm_o)
-    share(jnp.concatenate([total_of(R.all_a, 6 + n) for n in range(4)], axis=1), R.offsets_o)
-    share(total_of(R.all_a, 5), R.baseline_o)
+    def vectors():
+        share(total_of(R.all_a, 4), R.postnorm_o)
+        share(jnp.concatenate([total_of(R.all_a, 6 + n) for n in range(4)], axis=1), R.offsets_o)
+        share(total_of(R.all_a, 5), R.baseline_o)
+
+    def last():
+        share(total_of(R.all_b, 2), R.prenorm_o)
+        share(R.total[...], R.shifts_o)
+        eye = lax.broadcasted_iota(jnp.int32, (extent, extent), 0) == lax.broadcasted_iota(
+            jnp.int32, (extent, extent), 1
+        )
+        for yy in range(2):
+            back = jnp.broadcast_to(R.back[:, yy : yy + 1], (extent, extent))
+            row = column_sum(jnp.where(eye, back, 0.0))
+            cond = R.cond[yy : yy + 1, :]
+            gate = 1.0 / (1.0 + jnp.exp(-cond))
+            R.time_o[yy : yy + 1, :] = row * (gate * (1.0 + cond * (1.0 - gate)))
+
+    early = [transpose] + [functools.partial(section, n, h) for n in range(2, 6) for h in range(2)] + [vectors]
+    later = [functools.partial(section, n, h) for n in range(2) for h in range(2)] + [last]
+    return early, later
+
+
+def finish_kernel(count, *refs):
+    sums, others, refs = refs[:4], refs[4 : 4 + count], refs[4 + count :]
+    sum_outs, other_outs, refs = refs[:4], refs[4 : 4 + count], refs[4 + count :]
+    low, high, sem = refs[:4], refs[4:8], refs[8]
+    loads = [pltpu.make_async_copy(a, b, sem.at[n]) for n, (a, b) in enumerate(zip(sums, low))]
+    copies = [pltpu.make_async_copy(a, b, sem.at[8 + n]) for n, (a, b) in enumerate(zip(others, other_outs))]
+    stores = [pltpu.make_async_copy(a, b, sem.at[4 + n]) for n, (a, b) in enumerate(zip(high, sum_outs))]
+    for item in loads + copies:
+        item.start()
+    for n in range(4):
+        loads[n].wait()
+        high[n][...] = low[n][...].astype(F32)
+        stores[n].start()
+    for item in stores + copies:
+        item.wait()
+
+
+def finish(sums, others):
+    hbm = pl.BlockSpec(memory_space=pl.ANY)
+    shape = jax.ShapeDtypeStruct
+    return pl.pallas_call(
+        functools.partial(finish_kernel, len(others)),
+        out_shape=tuple(shape(v.shape, F32) for v in sums) + tuple(shape(v.shape, v.dtype) for v in others),
+        in_specs=[hbm] * (4 + len(others)),
+        out_specs=(hbm,) * (4 + len(others)),
+        scratch_shapes=[pltpu.VMEM(v.shape, BF16) for v in sums] + [pltpu.VMEM(v.shape, F32) for v in sums]
+        + [pltpu.SemaphoreType.DMA((8 + len(others),))],
+        compiler_params=pltpu.CompilerParams(vmem_limit_bytes=60 * 1024 * 1024),
+        name="finish",
+    )(*sums, *others)
 
 
 def rotary_constants(length):
@@ -935,7 +1016,6 @@
     out_shape = [
         shape(tokens.shape, BF16), shape(tokens.shape, BF16), shape((width // 8, ff), BF16),
         shape((ff // 8, width), BF16), shape((width // 8, width), BF16), shape((width // 8, 3 * width), BF16),
-        shape((2 * pairs * 4, span, total), BF16),
     ]
     out_specs = [hbm] * len(out_shape)
     names = INPUTS + GRADS
@@ -955,7 +1035,7 @@
     outs = pl.pallas_call(
         functools.partial(layer_kernel, leftover, names),
         out_shape=tuple(out_shape),
-        in_specs=[hbm] * 7 + [vmem] * 8,
+        in_specs=[hbm] * 15,
         out_specs=tuple(out_specs),
         scratch_shapes=list(buffers.values()),
         compiler_params=pltpu.CompilerParams(
@@ -967,13 +1047,17 @@
         condition, shifts, prenorm, postnorm, offsets, baseline, jnp.asarray(cosine), jnp.asarray(sine),
     )
     layer_output, grad_tokens = outs[0], outs[1]
-    grad_expand, grad_contract, grad_projection, grad_mixer = (part.astype(F32) for part in outs[2:6])
     if leftover == 1:
-        grad_time, grad_adaptive, grad_shifts, grad_prenorm, grad_postnorm, grad_offsets, grad_baseline = outs[7:]
+        done = finish(outs[2:6], outs[:2] + outs[6:])
+        grad_expand, grad_contract, grad_projection, grad_mixer = done[:4]
+        layer_output, grad_tokens = done[4:6]
+        grad_time, grad_adaptive, grad_shifts, grad_prenorm, grad_postnorm, grad_offsets, grad_baseline = done[6:]
         return (
             layer_output, grad_tokens, grad_time, grad_adaptive, grad_shifts, grad_prenorm, grad_mixer,
             grad_projection, grad_postnorm, grad_expand, grad_offsets, grad_contract, grad_baseline,
         )
+
+    grad_expand, grad_contract, grad_projection, grad_mixer = (part.astype(F32) for part in outs[2:6])
 
     w = lax.axis_index("wide")
 
@@ -986,10 +1070,9 @@
     grad_expand, grad_contract, grad_projection, grad_mixer = (
         among_groups(part) for part in (grad_expand, grad_contract, grad_projection, grad_mixer)
     )
-    all_a, all_b = outs[7], outs[8]
+    all_a, all_b = outs[6], outs[7]
     every = jnp.concatenate([all_b, all_a], axis=2)
-    every = every.transpose(1, 2, 0, 3).reshape(2, 8, 24, width)
-    every = every.transpose(1, 0, 2, 3)
+    every = every.reshape(2, 2, 2, 2, 2, 24, half).transpose(2, 3, 1, 4, 5, 0, 6).reshape(8, 2, 24, width)
     mine = lax.dynamic_slice_in_dim(every, lax.div(w, leftover), 1, axis=0)[0]
     every = lax.all_gather(mine, "wide", axis=0, tiled=True)
     sections = [0, 1, 8, 9, 10, 11]

time: 178 us -> 183 us (1.028)
  Pallas kernels: 163 us -> 182 us
  other arithmetic: 7.08 us -> 0 us
  local copies, waits for them, and re-layouts: 5.78 us -> 0 us
    pallas_call x0 -> x1, Pallas kernels: none -> 58.1 us  [finish(): pl.pallas_call(functools.partial(finish_kernel, len(others)), out_shape=t...]
    pallas_call x1, Pallas kernels: 163 us -> 124 us  [local_part(): pl.pallas_call(functools.partial(layer_kernel, leftover, names), out_shap...]
    convert_element_type x4 -> x0, other arithmetic: 7.08 us -> none  [local_part(): part.astype(F32)]
    unnamed x29 -> x0, local copies, waits for them, and re-layouts: 5.78 us -> none
where the time goes in v3:
time: 183 us
  Pallas kernels  182 us (99%)
    pallas_call x1, Pallas kernels, local_part(): pl.pallas_call(functools.partial(layer_kernel, leftover, names), out_shap...  124 us
    pallas_call x1, Pallas kernels, finish(): pl.pallas_call(functools.partial(finish_kernel, len(others)), out_shape=t...  58.1 us

profile of v3, /device:TPU:1, one launch (start us, length us, event | category | flops | bytes accessed | tf_op | source)
XLA Modules:
  0.0 182.8 jit_solution(2014200268784105281)
XLA Ops:
  0.6 123.9 %layer.1 = (bf16[2,256,768]{2,1,0:T(8,128)(2,1)}, bf16[2,256,768]{2,1,0:T(8,128)(2,1)}, bf16[96,3072]{1,0:T(8,128)(2,1)}, bf16[384,768]{1,0:T(8,128)(2,1)}, bf16...) custom-call(bf16[2,256,768]{2,1,0:T(8,128)(2,1)} %refs_0_.1, ...), custom_call_target="tpu_custom_call" | custom-call | tf_op jit(solution)/shard_map/layer/pallas_call | solution.py:1035
  124.6 58.1 %finish.1 = (f32[96,3072]{1,0:T(8,128)}, f32[384,768]{1,0:T(8,128)}, f32[96,768]{1,0:T(8,128)}, f32[96,2304]{1,0:T(8,128)}, bf16[2,256,768]{2,1,0:T(8,128)(2,1)}...) custom-call(bf16[96,3072]{1,0:T(8,128)(2,1)} %get-tuple-element.39.r, ...), custom_call_target="tpu_custom_call" | custom-call | tf_op jit(solution)/shard_map/finish/pallas_call | solution.py:979

commit v4 on v3

--- a/solution.py
+++ b/solution.py
@@ -957,19 +957,21 @@
 
 
 def finish_kernel(count, *refs):
-    sums, others, refs = refs[:4], refs[4 : 4 + count], refs[4 + count :]
-    sum_outs, other_outs, refs = refs[:4], refs[4 : 4 + count], refs[4 + count :]
-    low, high, sem = refs[:4], refs[4:8], refs[8]
-    loads = [pltpu.make_async_copy(a, b, sem.at[n]) for n, (a, b) in enumerate(zip(sums, low))]
-    copies = [pltpu.make_async_copy(a, b, sem.at[8 + n]) for n, (a, b) in enumerate(zip(others, other_outs))]
-    stores = [pltpu.make_async_copy(a, b, sem.at[4 + n]) for n, (a, b) in enumerate(zip(high, sum_outs))]
-    for item in loads + copies:
+    total = 4 + count
+    given, results, held, high, sem = (
+        refs[:total], refs[total : 2 * total], refs[2 * total : 3 * total], refs[3 * total : 3 * total + 4], refs[-1]
+    )
+    loads = [pltpu.make_async_copy(a, b, sem.at[n]) for n, (a, b) in enumerate(zip(given, held))]
+    written = tuple(high) + tuple(held[4:])
+    stores = [pltpu.make_async_copy(a, b, sem.at[total + n]) for n, (a, b) in enumerate(zip(written, results))]
+    for item in loads:
         item.start()
-    for n in range(4):
+    for n in range(total):
         loads[n].wait()
-        high[n][...] = low[n][...].astype(F32)
+        if n < 4:
+            high[n][...] = held[n][...].astype(F32)
         stores[n].start()
-    for item in stores + copies:
+    for item in stores:
         item.wait()
 
 
@@ -981,8 +983,8 @@
         out_shape=tuple(shape(v.shape, F32) for v in sums) + tuple(shape(v.shape, v.dtype) for v in others),
         in_specs=[hbm] * (4 + len(others)),
         out_specs=(hbm,) * (4 + len(others)),
-        scratch_shapes=[pltpu.VMEM(v.shape, BF16) for v in sums] + [pltpu.VMEM(v.shape, F32) for v in sums]
-        + [pltpu.SemaphoreType.DMA((8 + len(others),))],
+        scratch_shapes=[pltpu.VMEM(v.shape, v.dtype) for v in (*sums, *others)]
+        + [pltpu.VMEM(v.shape, F32) for v in sums] + [pltpu.SemaphoreType.DMA((8 + 2 * len(others),))],
         compiler_params=pltpu.CompilerParams(vmem_limit_bytes=60 * 1024 * 1024),
         name="finish",
     )(*sums, *others)

time: 183 us -> 129 us (0.70)
  Pallas kernels: 182 us -> 128 us
    pallas_call x1, Pallas kernels: 58.1 us -> 3.77 us  [finish(): pl.pallas_call(functools.partial(finish_kernel, len(others)), out_shape=t...]
where the time goes in v4:
time: 129 us
  Pallas kernels  128 us (99%)
    pallas_call x1, Pallas kernels, local_part(): pl.pallas_call(functools.partial(layer_kernel, leftover, names), out_shap...  124 us
    pallas_call x1, Pallas kernels, finish(): pl.pallas_call(functools.partial(finish_kernel, len(others)), out_shape=t...  3.77 us

profile of v4, /device:TPU:1, one launch (start us, length us, event | category | flops | bytes accessed | tf_op | source)
XLA Modules:
  0.0 128.5 jit_solution(11627908659648625465)
XLA Ops:
  0.6 123.9 %layer.1 = (bf16[2,256,768]{2,1,0:T(8,128)(2,1)}, bf16[2,256,768]{2,1,0:T(8,128)(2,1)}, bf16[96,3072]{1,0:T(8,128)(2,1)}, bf16[384,768]{1,0:T(8,128)(2,1)}, bf16...) custom-call(bf16[2,256,768]{2,1,0:T(8,128)(2,1)} %refs_0_.1, ...), custom_call_target="tpu_custom_call" | custom-call | tf_op jit(solution)/shard_map/layer/pallas_call | solution.py:1037
  124.6 3.8 %finish.1 = (f32[96,3072]{1,0:T(8,128)}, f32[384,768]{1,0:T(8,128)}, f32[96,768]{1,0:T(8,128)}, f32[96,2304]{1,0:T(8,128)}, bf16[2,256,768]{2,1,0:T(8,128)(2,1)}...) custom-call(bf16[96,3072]{1,0:T(8,128)(2,1)} %get-tuple-element.39.r, ...), custom_call_target="tpu_custom_call" | custom-call | tf_op jit(solution)/shard_map/finish/pallas_call | solution.py:981

commit v5 on v4

--- a/solution.py
+++ b/solution.py
@@ -964,9 +964,9 @@
     loads = [pltpu.make_async_copy(a, b, sem.at[n]) for n, (a, b) in enumerate(zip(given, held))]
     written = tuple(high) + tuple(held[4:])
     stores = [pltpu.make_async_copy(a, b, sem.at[total + n]) for n, (a, b) in enumerate(zip(written, results))]
-    for item in loads:
-        item.start()
-    for n in range(total):
+    for n in (0, 4, 1, 5, 3, 2, *range(6, total)):
+        loads[n].start()
+    for n in (0, 4, 1, 5, 3, 2, *range(6, total)):
         loads[n].wait()
         if n < 4:
             high[n][...] = held[n][...].astype(F32)

time: 129 us -> 129 us (level)
  no operation moved by 1% of the time
where the time goes in v5:
time: 129 us
  Pallas kernels  128 us (99%)
    pallas_call x1, Pallas kernels, local_part(): pl.pallas_call(functools.partial(layer_kernel, leftover, names), out_shap...  124 us
    pallas_call x1, Pallas kernels, finish(): pl.pallas_call(functools.partial(finish_kernel, len(others)), out_shape=t...  3.78 us

profile of v5, /device:TPU:1, one launch (start us, length us, event | category | flops | bytes accessed | tf_op | source)
XLA Modules:
  0.0 128.5 jit_solution(16876717119884480016)
XLA Ops:
  0.6 123.9 %layer.1 = (bf16[2,256,768]{2,1,0:T(8,128)(2,1)}, bf16[2,256,768]{2,1,0:T(8,128)(2,1)}, bf16[96,3072]{1,0:T(8,128)(2,1)}, bf16[384,768]{1,0:T(8,128)(2,1)}, bf16...) custom-call(bf16[2,256,768]{2,1,0:T(8,128)(2,1)} %refs_0_.1, ...), custom_call_target="tpu_custom_call" | custom-call | tf_op jit(solution)/shard_map/layer/pallas_call | solution.py:1037
  124.6 3.8 %finish.1 = (f32[96,3072]{1,0:T(8,128)}, f32[384,768]{1,0:T(8,128)}, f32[96,768]{1,0:T(8,128)}, f32[96,2304]{1,0:T(8,128)}, bf16[2,256,768]{2,1,0:T(8,128)(2,1)}...) custom-call(bf16[96,3072]{1,0:T(8,128)(2,1)} %get-tuple-element.39.r, ...), custom_call_target="tpu_custom_call" | custom-call | tf_op jit(solution)/shard_map/finish/pallas_call | solution.py:981
